TPU v7x, 32 devices: a whole 2x2x4 slice. The times are simulated.
32 devices in a mesh: img: 16 (over z, x, core), seq: 2 (over y).
Axes of the slice: x: 2, y: 2, z: 4, core: 2. Of those that a mesh axis runs over, the one named last changes fastest.
Arguments:
- patches: bfloat16 [64, 1024, 768], P('img', 'seq'), may hold values from -6 to 6
- lengths: int32 [64], P('img'), may hold values from 192 to 1024, as said below
- pooled_cot: float32 [64, 768], P('img'), may hold values from -6 to 6
- norm1_gain: bfloat16 [768], P(('img', 'seq')), may hold values from 0.5 to 1.5
- norm1_bias: bfloat16 [768], P(('img', 'seq')), may hold values from -1.75 to 1.75
- qkv_weight: bfloat16 [768, 2304], P(('img', 'seq')), may hold values from -0.21875 to 0.21875
- query_bias: bfloat16 [768], P(('img', 'seq')), may hold values from -1.75 to 1.75
- value_bias: bfloat16 [768], P(('img', 'seq')), may hold values from -1.75 to 1.75
- attn_weight: bfloat16 [768, 768], P(('img', 'seq')), may hold values from -1.25 to 1.25
- attn_bias: bfloat16 [768], P(('img', 'seq')), may hold values from -1.75 to 1.75
- norm2_gain: bfloat16 [768], P(('img', 'seq')), may hold values from 0.5 to 1.5
- norm2_bias: bfloat16 [768], P(('img', 'seq')), may hold values from -1.75 to 1.75
- fc1_weight: bfloat16 [768, 3072], P(('img', 'seq')), may hold values from -0.21875 to 0.21875
- fc1_bias: bfloat16 [3072], P(('img', 'seq')), may hold values from -1.75 to 1.75
- fc2_weight: bfloat16 [3072, 768], P(('img', 'seq')), may hold values from -0.109375 to 0.109375
- fc2_bias: bfloat16 [768], P(('img', 'seq')), may hold values from -1.75 to 1.75
- final_gain: bfloat16 [768], P(('img', 'seq')), may hold values from 0.5 to 1.5
- final_bias: bfloat16 [768], P(('img', 'seq')), may hold values from -1.75 to 1.75
- probe_vector: bfloat16 [768], P(('img', 'seq')), may hold values from -6 to 6
- pool_query_weight: bfloat16 [768, 768], P(('img', 'seq')), may hold values from -0.21875 to 0.21875
- pool_query_bias: bfloat16 [768], P(('img', 'seq')), may hold values from -1.75 to 1.75
- pool_kv_weight: bfloat16 [768, 1536], P(('img', 'seq')), may hold values from -0.21875 to 0.21875
- pool_value_bias: bfloat16 [768], P(('img', 'seq')), may hold values from -1.75 to 1.75
- pool_out_weight: bfloat16 [768, 768], P(('img', 'seq')), may hold values from -1.25 to 1.25
- pool_out_bias: bfloat16 [768], P(('img', 'seq')), may hold values from -1.75 to 1.75
- head_gain: bfloat16 [768], P(('img', 'seq')), may hold values from 0.5 to 1.5
- head_bias: bfloat16 [768], P(('img', 'seq')), may hold values from -1.75 to 1.75
- head_fc1_weight: bfloat16 [768, 3072], P(('img', 'seq')), may hold values from -0.21875 to 0.21875
- head_fc1_bias: bfloat16 [3072], P(('img', 'seq')), may hold values from -1.75 to 1.75
- head_fc2_weight: bfloat16 [3072, 768], P(('img', 'seq')), may hold values from -0.109375 to 0.109375
- head_fc2_bias: bfloat16 [768], P(('img', 'seq')), may hold values from -1.75 to 1.75
Outputs:
- pooled: float32 [64, 768], P('img')
- patch_grad: float32 [64, 1024, 768], P('img', 'seq')
- grad_norm1_gain: float32 [768], P(('img', 'seq'))
- grad_norm1_bias: float32 [768], P(('img', 'seq'))
- grad_qkv_weight: float32 [768, 2304], P(('img', 'seq'))
- grad_query_bias: float32 [768], P(('img', 'seq'))
- grad_value_bias: float32 [768], P(('img', 'seq'))
- grad_attn_weight: float32 [768, 768], P(('img', 'seq'))
- grad_attn_bias: float32 [768], P(('img', 'seq'))
- grad_norm2_gain: float32 [768], P(('img', 'seq'))
- grad_norm2_bias: float32 [768], P(('img', 'seq'))
- grad_fc1_weight: float32 [768, 3072], P(('img', 'seq'))
- grad_fc1_bias: float32 [3072], P(('img', 'seq'))
- grad_fc2_weight: float32 [3072, 768], P(('img', 'seq'))
- grad_fc2_bias: float32 [768], P(('img', 'seq'))
- grad_final_gain: float32 [768], P(('img', 'seq'))
- grad_final_bias: float32 [768], P(('img', 'seq'))
- grad_probe_vector: float32 [768], P(('img', 'seq'))
- grad_pool_query_weight: float32 [768, 768], P(('img', 'seq'))
- grad_pool_query_bias: float32 [768], P(('img', 'seq'))
- grad_pool_kv_weight: float32 [768, 1536], P(('img', 'seq'))
- grad_pool_value_bias: float32 [768], P(('img', 'seq'))
- grad_pool_out_weight: float32 [768, 768], P(('img', 'seq'))
- grad_pool_out_bias: float32 [768], P(('img', 'seq'))
- grad_head_gain: float32 [768], P(('img', 'seq'))
- grad_head_bias: float32 [768], P(('img', 'seq'))
- grad_head_fc1_weight: float32 [768, 3072], P(('img', 'seq'))
- grad_head_fc1_bias: float32 [3072], P(('img', 'seq'))
- grad_head_fc2_weight: float32 [3072, 768], P(('img', 'seq'))
- grad_head_fc2_bias: float32 [768], P(('img', 'seq'))
Inputs may be any that keep to these rules, and one draw needn't show every extreme that they name: `lengths`: valid patches of each image; positions from the count on are padding.
All inputs are finite; a program needn't handle non-finite values.
Results may differ from a plain program's by a relative error of at most 0.024.
Values may be sent and summed in bfloat16 or wider, within the bound.
No kernel may reach another device: no remote copies, remote signals or barrier semaphores. Data moves between devices by JAX's collectives and lax.ppermute only.
A program may use at most 320 MiB of HBM per device.

v0:
```python
import functools

import jax
import jax.numpy as jnp
from jax import lax
from jax.experimental import pallas as pl
from jax.experimental.pallas import tpu as pltpu
from jax.sharding import PartitionSpec as P

HEADS = 12
HEAD_DIM = 64
BLOCK = 256
PAIR = 128
wide = jnp.float32
low = jnp.bfloat16
masked_score = -1e30
norm_epsilon = 1e-06
root_two_pi = 0.7978845608028654
vmem_bytes = 60 * 1024 * 1024


def dot_nn(a, b):
    return jnp.dot(a, b, preferred_element_type=wide)


def dot_nt(a, b):
    return lax.dot_general(a, b, (((1,), (1,)), ((), ())), preferred_element_type=wide)


def dot_tn(a, b):
    return lax.dot_general(a, b, (((0,), (0,)), ((), ())), preferred_element_type=wide)


def halves(v):
    top = v.astype(low)
    return top, (v - top.astype(wide)).astype(low)


def normalise(v):
    centred = v - jnp.mean(v, axis=-1, keepdims=True)
    spread = jnp.mean(centred * centred, axis=-1, keepdims=True)
    scale = lax.rsqrt(spread + norm_epsilon)
    return centred * scale, scale


def norm_back(grad, gain, normal, scale):
    gn = grad * gain
    return (
        gn
        - jnp.mean(gn, axis=-1, keepdims=True)
        - normal * jnp.mean(gn * normal, axis=-1, keepdims=True)
    ) * scale


def column_sum(v):
    return jnp.sum(v, axis=0, keepdims=True)


def params(rank):
    return pltpu.CompilerParams(
        dimension_semantics=("arbitrary",) * rank, vmem_limit_bytes=vmem_bytes
    )


def whole(shape):
    return pl.BlockSpec(
        shape, lambda *_: (0,) * len(shape), pipeline_mode=pl.Buffered(1)
    )


def cost(flops, nbytes, exps=0):
    return pl.CostEstimate(flops=int(flops), bytes_accessed=int(nbytes), transcendentals=int(exps))


class Sizes:
    def __init__(self, images, length, width, hidden):
        self.images, self.length, self.width, self.hidden = images, length, width, hidden
        self.rows = images * length
        self.blocks = length // BLOCK
        self.pairs = width // PAIR

        self.units = 0

    def row_spec(self, cols):
        blocks = self.blocks

        def index(i, b, meta):
            return i * blocks + jnp.clip(b, 0, jnp.maximum(meta[i] - 1, 0)), 0

        return pl.BlockSpec((BLOCK, cols), index)

    def lane_spec(self, rows):
        def index(i, b, meta):
            return i, 0, jnp.clip(b, 0, jnp.maximum(meta[i] - 1, 0))

        return pl.BlockSpec((1, rows, BLOCK), index)

    def image_spec(self, rows, cols):
        return pl.BlockSpec((1, rows, cols), lambda i, b, meta: (i, 0, 0))


(
    NORM1_GAIN,
    NORM1_BIAS,
    QUERY_BIAS,
    VALUE_BIAS,
    ATTN_BIAS,
    NORM2_GAIN,
    NORM2_BIAS,
    FC2_BIAS,
    FINAL_GAIN,
    FINAL_BIAS,
    POOL_QUERY_BIAS,
    POOL_VALUE_BIAS,
    POOL_OUT_BIAS,
    HEAD_GAIN,
    HEAD_BIAS,
    HEAD_FC2_BIAS,
) = range(16)


PROBE = 16
FC1_BIAS = 17
VECTORS = 32


def row_of(ref, at):
    return ref[at : at + 1, :]


anywhere = pl.BlockSpec(memory_space=pl.ANY)


def fetch_all(meta, base, parts, held, sems):
    copies, place = [], 0
    for part in parts:
        for k in range(part.shape[0]):
            copies.append(
                pltpu.make_async_copy(part.at[k], held.at[meta[base + place]], sems.at[place])
            )
            place += 1
    for copy in copies:
        copy.start()
    for copy in copies:
        copy.wait()


def held_scratch(parts):
    units = sum(part.shape[0] for part in parts)
    return [
        pltpu.VMEM((units,) + parts[0].shape[1:], parts[0].dtype),
        pltpu.SemaphoreType.DMA((units,)),
    ]


def columns(held, start, size):
    units, rows, _ = held.shape
    return held[:, :, start : start + size].reshape(units * rows, size)


def is_first():
    return (pl.program_id(0) == 0) & (pl.program_id(1) == 0)


def packs_body(count, *refs):
    rows = refs[:count]
    qkv, pool_kv, pool_query, attn, fc1, fc2, pool_out, head_fc1, head_fc2 = refs[count:-4]
    first, block, head, lines = refs[-4:]
    own, width = attn.shape
    fold = fc1.shape[1] // width
    chunk = fold * PAIR
    at_from = lax.broadcasted_iota(jnp.int32, (chunk, chunk), 0)
    at_to = lax.broadcasted_iota(jnp.int32, (chunk, chunk), 1)
    spread = jnp.where(at_from == (at_to % PAIR) * fold + at_to // PAIR, 1.0, 0.0).astype(low)
    row_from = lax.broadcasted_iota(jnp.int32, (own, own * fold), 1)
    row_to = lax.broadcasted_iota(jnp.int32, (own, own * fold), 0)

    def by_part(ref, out, start):
        for k in range(width // PAIR):
            value = dot_nn(ref[:, k * chunk : (k + 1) * chunk], spread).astype(low)
            for j in range(fold):
                to = start + j * width + k * PAIR
                out[:, to : to + PAIR] = value[:, j * PAIR : (j + 1) * PAIR]

    def by_row(ref, out, start):
        for j in range(fold):
            pick = jnp.where(row_from == row_to * fold + j, 1.0, 0.0).astype(low)
            to = start + j * width
            out[:, to : to + width] = dot_nn(pick, ref[...]).astype(low)

    lines[...] = jnp.zeros_like(lines)
    at = 0
    for ref in rows:
        lines[at : at + ref.shape[0], :own] = ref[...].astype(wide)
        at += ref.shape[0]
    first[:, : 3 * width] = qkv[...]
    first[:, 3 * width :] = lines[...].T[:own].astype(low)
    block[:, : 2 * width] = pool_kv[...]
    block[:, 2 * width : 3 * width] = pool_query[...]
    block[:, 3 * width : 4 * width] = pool_out[...]
    block[:, 4 * width : 5 * width] = attn[...]
    by_part(fc1, block, 5 * width)
    by_row(fc2, block, (5 + fold) * width)
    by_part(head_fc1, head, 0)
    by_row(head_fc2, head, fold * width)


def packs_call(rows, *weights):
    own, width = weights[3].shape
    fold = weights[4].shape[1] // width
    ins = (*rows, *weights)
    vmem = pl.BlockSpec(memory_space=pltpu.VMEM)
    return pl.pallas_call(
        functools.partial(packs_body, len(rows)),
        in_specs=[vmem] * len(ins),
        out_specs=[vmem] * 3,
        out_shape=[
            jax.ShapeDtypeStruct((own, cols), low)
            for cols in (3 * width + PAIR, (5 + 2 * fold) * width, 2 * fold * width)
        ],
        scratch_shapes=[pltpu.VMEM((PAIR, PAIR), wide)],
        compiler_params=params(0),
        cost_estimate=cost(0, 4 * own * width * (9 + 4 * fold)),
        name="packs",
    )(*ins)


def qkv_body(base, meta, x, mine, theirs, qkv, normed, vec, held, sems):
    width = x.shape[1]

    @pl.when(is_first())
    def _():
        fetch_all(meta, base, (mine, theirs), held, sems)
        vec[...] = columns(held, 3 * width, PAIR).astype(wide).T[:VECTORS]

    @pl.when(pl.program_id(1) < meta[pl.program_id(0)])
    def _():
        normal, _ = normalise(x[...].astype(wide))
        rows = (normal * row_of(vec, NORM1_GAIN) + row_of(vec, NORM1_BIAS)).astype(low)
        normed[...] = rows
        for part, bias in enumerate((QUERY_BIAS, None, VALUE_BIAS)):
            out = dot_nn(rows, columns(held, part * width, width))
            if bias is not None:
                out = out + row_of(vec, bias)
            qkv[:, part * width : (part + 1) * width] = out.astype(low)


def qkv_call(sz, meta, x, weight):
    w = sz.width
    return pl.pallas_call(
        functools.partial(qkv_body, 2 * sz.images),
        grid_spec=pltpu.PrefetchScalarGridSpec(
            num_scalar_prefetch=1,
            grid=(sz.images, sz.blocks),
            in_specs=[sz.row_spec(w), anywhere, anywhere],
            out_specs=[
                sz.row_spec(3 * w),
                sz.row_spec(w),
                pl.BlockSpec((VECTORS, w), lambda i, b, m: (0, 0)),
            ],
            scratch_shapes=held_scratch(weight),
        ),
        out_shape=[
            jax.ShapeDtypeStruct((sz.rows, 3 * w), low),
            jax.ShapeDtypeStruct((sz.rows, w), low),
            jax.ShapeDtypeStruct((VECTORS, w), wide),
        ],
        compiler_params=params(2),
        cost_estimate=cost(6 * sz.rows * w * w, sz.rows * w * 10 + 6 * w * w),
        name="qkv",
    )(meta, x, *weight)


def attend_body(images, blocks, at, meta, q_ref, k_ref, v_ref, *rest):
    out_ref, lse_ref = rest[-2:]
    count, length = meta[at], meta[images + at]
    lane = lax.broadcasted_iota(jnp.int32, (BLOCK, PAIR), 1)
    first = lane < HEAD_DIM

    def variant(keys_in):
        near = keys_in - BLOCK
        column = lax.broadcasted_iota(jnp.int32, (BLOCK, BLOCK), 1) + near

        @pl.loop(0, count)
        def _(step):
            rows = pl.ds(pl.multiple_of(step * BLOCK, BLOCK), BLOCK)
            q = q_ref[rows, :]
            outs, logs = [], []
            for head in range(2):
                own = first if head == 0 else jnp.logical_not(first)
                qh = jnp.where(own, q, jnp.zeros_like(q))
                last = dot_nt(qh, k_ref[near:keys_in, :]) * 0.125
                last = jnp.where(column < length, last, masked_score)
                top = jnp.max(last, axis=1, keepdims=True)
                if near:
                    body = dot_nt(qh, k_ref[:near, :]) * 0.125
                    top = jnp.maximum(top, jnp.max(body, axis=1, keepdims=True))
                p_last = jnp.exp(last - top)
                total = jnp.sum(p_last, axis=1, keepdims=True)
                acc = dot_nn(p_last.astype(low), v_ref[near:keys_in, :])
                if near:
                    p_body = jnp.exp(body - top)
                    total = total + jnp.sum(p_body, axis=1, keepdims=True)
                    acc = acc + dot_nn(p_body.astype(low), v_ref[:near, :])
                outs.append(acc / total)
                logs.append(top + jnp.log(total))
            out_ref[rows, :] = jnp.where(first, outs[0], outs[1]).astype(low)
            both = jnp.where(lane == 0, logs[0], logs[1])
            lse_ref[0, :, rows] = both.T[:8, :]

    for keys in range(1, blocks + 1):
        pl.when(count == keys)(functools.partial(variant, keys * BLOCK))


def attend_call(sz, meta, qkv, at, before):
    pairs = sz.pairs

    def spec(part):
        return pl.BlockSpec((sz.length, PAIR), lambda p, m: (at, part * pairs + p))

    return pl.pallas_call(
        functools.partial(attend_body, sz.images, sz.blocks, at),
        grid_spec=pltpu.PrefetchScalarGridSpec(
            num_scalar_prefetch=1,
            grid=(pairs,),
            in_specs=[spec(0), spec(1), spec(2)] + [anywhere] * len(before),
            out_specs=[
                pl.BlockSpec((sz.length, PAIR), lambda p, m: (at, p)),
                pl.BlockSpec((1, 8, sz.length), lambda p, m: (at, p, 0)),
            ],
        ),
        out_shape=[
            jax.ShapeDtypeStruct((sz.rows, sz.width), low),
            jax.ShapeDtypeStruct((sz.images, 8 * pairs, sz.length), wide),
        ],
        input_output_aliases={4 + k: k for k in range(len(before))},
        compiler_params=params(1),
        cost_estimate=cost(
            4 * sz.length * sz.length * sz.width,
            8 * sz.length * sz.width,
            sz.length * sz.length * HEADS,
        ),
        name=f"attend_{at}",
    )(meta, qkv, qkv, qkv, *before)


AHEAD = 4


def mlp_body(meta, x, att, vec, weight, res, n2, slope, act, enc, fin):
    @pl.when(pl.program_id(1) < meta[pl.program_id(0)])
    def _():
        width = x.shape[1]
        fold = slope.shape[1] // width

        def part_of(k):
            return weight[:, (AHEAD + k) * width : (AHEAD + k + 1) * width]

        branch = dot_nn(att[...], part_of(0)) + row_of(vec, ATTN_BIAS)
        rows = x[...].astype(wide) + branch
        res[...] = rows
        normal, _ = normalise(rows)
        normed = (normal * row_of(vec, NORM2_GAIN) + row_of(vec, NORM2_BIAS)).astype(low)
        n2[...] = normed
        total = rows + row_of(vec, FC2_BIAS)
        for part in range(fold):
            cols = slice(part * width, (part + 1) * width)
            u = dot_nn(normed, part_of(1 + part)) + row_of(vec, FC1_BIAS + part)
            square = u * u
            bend = jnp.tanh(root_two_pi * u * (1.0 + 0.044715 * square))
            half = 0.5 * (1.0 + bend)
            hidden = (u * half).astype(low)
            slope[:, cols] = (
                half
                + (0.5 * root_two_pi) * u * (1.0 - bend * bend) * (1.0 + 0.134145 * square)
            ).astype(low)
            act[:, cols] = hidden
            total = total + dot_nn(hidden, part_of(1 + fold + part))
        enc[...] = total
        normal, _ = normalise(total)
        fin[...] = (normal * row_of(vec, FINAL_GAIN) + row_of(vec, FINAL_BIAS)).astype(low)


def mlp_call(sz, meta, x, att, vec, weight):
    w, f = sz.width, sz.hidden
    return pl.pallas_call(
        mlp_body,
        grid_spec=pltpu.PrefetchScalarGridSpec(
            num_scalar_prefetch=1,
            grid=(sz.images, sz.blocks),
            in_specs=[sz.row_spec(w), sz.row_spec(w), whole(vec.shape), whole(weight.shape)],
            out_specs=[sz.row_spec(c) for c in (w, w, f, f, w, w)],
        ),
        out_shape=[
            jax.ShapeDtypeStruct((sz.rows, w), wide),
            jax.ShapeDtypeStruct((sz.rows, w), low),
            jax.ShapeDtypeStruct((sz.rows, f), low),
            jax.ShapeDtypeStruct((sz.rows, f), low),
            jax.ShapeDtypeStruct((sz.rows, w), wide),
            jax.ShapeDtypeStruct((sz.rows, w), low),
        ],
        compiler_params=params(2),
        cost_estimate=cost(
            sz.rows * w * (2 * w + 4 * f), sz.rows * (14 * w + 4 * f) + 4 * w * f, sz.rows * f
        ),
        name="mlp",
    )(meta, x, att, vec, weight)


HEAD_ROWS = 16


SENT_ROWS = 48
SENT_MIX, SENT_ACT, SENT_GRAD, SENT_NORMED, SENT_POOLED = 16, 32, 36, 40, 41
SENT_BRANCH, SENT_PULL, SENT_COT, SENT_OUT, SENT_OUT_REST = 42, 43, 44, 45, 46
SENT_QUERY, SENT_QUERY_REST = 47, 31


def head_body(
    images, blocks, fold, meta, fin, cot_ref, vec, pool_w, mine, theirs, rest,
    shares, g_score, lift, probe_out, sent, sums, score, mixed, line, held, sems,
):
    width = fin.shape[1]
    fetch_all(meta, 2 * images, (mine, theirs, rest), held, sems)
    keys_w, values_w, query_w, out_w = (
        pool_w.at[:, k * width : (k + 1) * width] for k in range(AHEAD)
    )

    def part_of(k):
        return columns(held, k * width, width)

    head_row = lax.broadcasted_iota(jnp.int32, (HEAD_ROWS, width), 0)
    head_col = lax.broadcasted_iota(jnp.int32, (HEAD_ROWS, width), 1) // HEAD_DIM
    own = head_row == head_col
    row_id = lax.broadcasted_iota(jnp.int32, (HEAD_ROWS, 1), 0)
    probe = jnp.broadcast_to(row_of(vec, PROBE), (HEAD_ROWS, width)).astype(low)
    query = (dot_nn(probe, query_w[...]) + row_of(vec, POOL_QUERY_BIAS)).astype(low)
    probe_w = 0.125 * dot_nt(jnp.where(own, query, jnp.zeros_like(query)), keys_w[...])
    probe_out[...] = jnp.where(row_id == HEADS, query.astype(wide), probe_w)
    probe_top, probe_rest = halves(probe_w)
    pooled_heads = jnp.zeros((HEAD_ROWS, width), wide)

    def block_rows(i, b):
        start = (i * blocks + b) * BLOCK
        return fin[start : start + BLOCK, :]

    for i in range(images):
        count, length = meta[i], meta[images + i]
        for b in range(blocks):
            cols = slice(b * BLOCK, (b + 1) * BLOCK)
            score[:, cols] = jnp.full((HEAD_ROWS, BLOCK), masked_score, wide)

            @pl.when(b < count)
            def _(i=i, b=b, cols=cols, length=length):
                rows = block_rows(i, b)
                value = dot_nt(probe_top, rows) + dot_nt(probe_rest, rows)
                column = lax.broadcasted_iota(jnp.int32, (HEAD_ROWS, BLOCK), 1) + b * BLOCK
                score[:, cols] = jnp.where(column < length, value, masked_score)

        raised = jnp.exp(score[...] - jnp.max(score[...], axis=1, keepdims=True))
        shares[i] = raised / jnp.sum(raised, axis=1, keepdims=True)
        mixed[i] = jnp.zeros((HEAD_ROWS, width), wide)
        for b in range(blocks):
            cols = slice(b * BLOCK, (b + 1) * BLOCK)

            @pl.when(b < count)
            def _(i=i, b=b, cols=cols):
                rows = block_rows(i, b)
                top, rest = halves(shares[i, :, cols])
                mixed[i] += dot_nn(top, rows) + dot_nn(rest, rows)

        top, rest = halves(mixed[i])
        sent[i * SENT_ROWS : i * SENT_ROWS + HEAD_ROWS, :] = top
        heads = dot_nn(top, values_w[...]) + dot_nn(rest, values_w[...])
        row = column_sum(jnp.where(own, heads, 0.0)) + row_of(vec, POOL_VALUE_BIAS)
        pooled_heads = jnp.where(row_id == i, row, pooled_heads)
    real = row_id < jnp.where(meta[0] > 0, images, 0)
    cot = jnp.where(real, cot_ref[...], 0.0)
    pooled_low = pooled_heads.astype(low)
    branch = dot_nn(pooled_low, out_w[...]) + row_of(vec, POOL_OUT_BIAS)
    normal, scale = normalise(branch)
    gain = row_of(vec, HEAD_GAIN)
    normed = (normal * gain + row_of(vec, HEAD_BIAS)).astype(low)
    cot_low = cot.astype(low)
    total = branch + row_of(vec, HEAD_FC2_BIAS)
    back = jnp.zeros((HEAD_ROWS, width), wide)

    def keep(at, value):
        for i in range(images):
            line[i, at - 2 * HEAD_ROWS : at + 1 - 2 * HEAD_ROWS, :] = value[i : i + 1, :].astype(wide)

    for part in range(fold):
        u = dot_nn(normed, part_of(part)) + row_of(vec, FC1_BIAS + fold + part)
        square = u * u
        bend = jnp.tanh(root_two_pi * u * (1.0 + 0.044715 * square))
        half = 0.5 * (1.0 + bend)
        act = (u * half).astype(low)
        slope = half + (0.5 * root_two_pi) * u * (1.0 - bend * bend) * (1.0 + 0.134145 * square)
        second = part_of(fold + part)
        total = total + dot_nn(act, second)
        grad = jnp.where(real, dot_nt(cot_low, second) * slope, 0.0).astype(low)
        back = back + dot_nt(grad, part_of(part))
        keep(SENT_ACT + part, act)
        keep(SENT_GRAD + part, grad)
    sums[...] = jnp.zeros_like(sums)
    sums[0:1, :] = column_sum(jnp.where(real, back * normal, 0.0))
    sums[1:2, :] = column_sum(jnp.where(real, back, 0.0))
    branch_grad = jnp.where(real, cot + norm_back(back, gain, normal, scale), 0.0).astype(low)
    pull = dot_nt(branch_grad, out_w[...])
    keep(SENT_NORMED, normed)
    keep(SENT_POOLED, pooled_low)
    keep(SENT_BRANCH, branch_grad)
    keep(SENT_PULL, pull)
    keep(SENT_COT, cot_low)
    top, rest = halves(total)
    keep(SENT_OUT, top)
    keep(SENT_OUT_REST, rest)
    for i in range(images):
        top, rest = halves(jnp.where(own, pull[i : i + 1, :], 0.0))
        raised = dot_nt(top, values_w[...]) + dot_nt(rest, values_w[...])
        drop = jnp.sum(raised * mixed[i], axis=1, keepdims=True)
        lift[i] = raised
        lift_top, lift_rest = halves(raised)
        mixed[i] = jnp.zeros((HEAD_ROWS, width), wide)
        for b in range(blocks):
            cols = slice(b * BLOCK, (b + 1) * BLOCK)

            @pl.when(b < meta[i])
            def _(i=i, b=b, cols=cols):
                rows = block_rows(i, b)
                reach = dot_nt(lift_top, rows) + dot_nt(lift_rest, rows)
                grad = shares[i, :, cols] * (reach - drop)
                g_score[i, :, cols] = grad
                top, rest = halves(grad)
                mixed[i] += dot_nn(top, rows) + dot_nn(rest, rows)

        top, rest = halves(mixed[i])
        pulled = dot_nn(top, keys_w[...]) + dot_nn(rest, keys_w[...])
        query_grad = 0.125 * column_sum(jnp.where(own, pulled, 0.0))
        query_top, query_rest = halves(query_grad)
        line[i, HEAD_ROWS - 1 : HEAD_ROWS, :] = query_top.astype(wide)
        both = jnp.where(row_id == HEAD_ROWS - 1, query_rest.astype(wide), mixed[i])
        start = i * SENT_ROWS + HEAD_ROWS
        sent[start : start + HEAD_ROWS, :] = both.astype(low)
        sent[start + HEAD_ROWS : start + 2 * HEAD_ROWS, :] = line[i].astype(low)


def head_call(sz, meta, fin, cot, vec, block, weight):
    w, f, n = sz.width, sz.hidden, sz.images

    def out(shape, dtype):
        return jax.ShapeDtypeStruct(shape, dtype)

    shapes = [
        out((n, HEAD_ROWS, sz.length), wide),
        out((n, HEAD_ROWS, sz.length), wide),
        out((n, HEAD_ROWS, w), wide),
        out((HEAD_ROWS, w), wide),
        out((n * SENT_ROWS, w), low),
        out((8, w), wide),
    ]
    ins = (fin, cot, vec)
    return pl.pallas_call(
        functools.partial(head_body, sz.images, sz.blocks, f // w),
        grid_spec=pltpu.PrefetchScalarGridSpec(
            num_scalar_prefetch=1,
            grid=(1,),
            in_specs=[whole(v.shape) for v in ins]
            + [pl.BlockSpec((w, AHEAD * w), lambda *_: (0, 0), pipeline_mode=pl.Buffered(1))]
            + [anywhere] * 3,
            out_specs=[pl.BlockSpec(s.shape, lambda *_, r=len(s.shape): (0,) * r) for s in shapes],
            scratch_shapes=[
                pltpu.VMEM((HEAD_ROWS, sz.length), wide),
                pltpu.VMEM((n, HEAD_ROWS, w), wide),
                pltpu.VMEM((n, HEAD_ROWS, w), wide),
            ]
            + held_scratch(weight),
        ),
        out_shape=shapes,
        compiler_params=params(1),
        cost_estimate=cost(16 * 8 * w * f, sz.rows * w * 2 + 4 * w * f + 8 * w * w),
        name="head",
    )(meta, *ins, block, *weight)


def back_body(
    meta, fin, enc, res, att, slope, g_score, shares, lift, probe_w, spread, vec, weight,
    g_mlp, g_hidden, g_res, g_branch, g_att, delta, sums,
):
    @pl.when(is_first())
    def _():
        sums[...] = jnp.zeros_like(sums)

    @pl.when(pl.program_id(1) < meta[pl.program_id(0)])
    def _():
        width = fin.shape[1]
        fold = slope.shape[1] // width

        def part_of(k):
            return weight[:, (AHEAD + k) * width : (AHEAD + k + 1) * width]

        lift_top, lift_rest = halves(lift[0])
        probe_top, probe_rest = halves(probe_w[...])
        top, rest = halves(g_score[0])
        share_top, share_rest = halves(shares[0])
        left = jnp.concatenate([top, share_top, rest, share_rest, top, share_top], axis=0)
        right = jnp.concatenate(
            [probe_top, lift_top, probe_top, lift_top, probe_rest, lift_rest], axis=0
        )
        g_fin = dot_tn(left, right)
        normal, scale = normalise(enc[...])
        sums[0:1, :] += column_sum(g_fin * normal)
        sums[1:2, :] += column_sum(g_fin)
        g_enc = norm_back(g_fin, row_of(vec, FINAL_GAIN), normal, scale)
        low_enc = g_enc.astype(low)
        g_mlp[...] = low_enc
        sums[2:3, :] += column_sum(low_enc.astype(wide))
        back = jnp.zeros_like(g_enc)
        for part in range(fold):
            cols = slice(part * width, (part + 1) * width)
            grad = dot_nt(low_enc, part_of(1 + fold + part))
            grad = (grad * slope[:, cols].astype(wide)).astype(low)
            g_hidden[:, cols] = grad
            sums[8 + part : 9 + part, :] += column_sum(grad.astype(wide))
            back = back + dot_nt(grad, part_of(1 + part))
        normal, scale = normalise(res[...])
        sums[3:4, :] += column_sum(back * normal)
        sums[4:5, :] += column_sum(back)
        total = g_enc + norm_back(back, row_of(vec, NORM2_GAIN), normal, scale)
        g_res[...] = total
        low_res = total.astype(low)
        g_branch[...] = low_res
        sums[5:6, :] += column_sum(low_res.astype(wide))
        grad = dot_nt(low_res, part_of(0)).astype(low)
        g_att[...] = grad
        top, rest = halves(grad.astype(wide) * att[...].astype(wide))
        delta[0] = dot_nt(spread[...], top) + dot_nt(spread[...], rest)


def back_call(
    sz, meta, fin, enc, res, att, slope, g_score, shares, lift, probe_w, vec, weight
):
    w, f, n = sz.width, sz.hidden, sz.images
    lines = 8 * sz.pairs
    line = lax.broadcasted_iota(jnp.int32, (lines, w), 0)
    head = lax.broadcasted_iota(jnp.int32, (lines, w), 1) // HEAD_DIM
    spread = (head == 2 * (line // 8) + line % 8).astype(low)
    fixed = (probe_w, spread, vec, weight)

    def out(shape, dtype):
        return jax.ShapeDtypeStruct(shape, dtype)

    def kept(shape):
        return pl.BlockSpec(shape, lambda i, b, m: (0, 0))

    return pl.pallas_call(
        back_body,
        grid_spec=pltpu.PrefetchScalarGridSpec(
            num_scalar_prefetch=1,
            grid=(n, sz.blocks),
            in_specs=[
                sz.row_spec(w), sz.row_spec(w), sz.row_spec(w), sz.row_spec(w), sz.row_spec(f),
                sz.lane_spec(HEAD_ROWS), sz.lane_spec(HEAD_ROWS), sz.image_spec(HEAD_ROWS, w),
            ]
            + [whole(v.shape) for v in fixed],
            out_specs=[
                sz.row_spec(w), sz.row_spec(f), sz.row_spec(w), sz.row_spec(w), sz.row_spec(w),
                sz.lane_spec(lines), kept((16, w)),
            ],
        ),
        out_shape=[
            out((sz.rows, w), low), out((sz.rows, f), low), out((sz.rows, w), wide),
            out((sz.rows, w), low), out((sz.rows, w), low), out((n, lines, sz.length), wide),
            out((16, w), wide),
        ],
        compiler_params=params(2),
        cost_estimate=cost(
            sz.rows * w * (2 * w + 4 * f), sz.rows * (22 * w + 4 * f) + 4 * w * f
        ),
        name="mlp_back",
    )(meta, fin, enc, res, att, slope, g_score, shares, lift, *fixed)


def outer_body(images, blocks, units, meta, a_ref, b_ref, out_ref, acc):
    span = blocks * BLOCK

    def finish(term):
        if units == 0:
            out_ref[...] = term.astype(out_ref.dtype)
            return
        rows = term.shape[0] // units
        for u in range(units):
            out_ref[meta[2 * images + units + u]] = term[u * rows : (u + 1) * rows].astype(low)

    for i in range(images):
        for keys in range(blocks + 1):

            @pl.when(meta[i] == keys)
            def _(i=i, keys=keys):
                if keys:
                    rows = slice(i * span, i * span + keys * BLOCK)
                    term = dot_tn(a_ref[rows, :], b_ref[rows, :])
                else:
                    term = jnp.zeros(acc.shape, wide)
                if i > 0:
                    term = term + acc[...]
                if i < images - 1:
                    acc[...] = term
                else:
                    finish(term)


def outer_block_body(
    images, blocks, fold, meta, att_ref, g_att_ref, n2_ref, g_hidden_ref, act_ref, g_mlp_ref, out_ref, acc
):
    step = pl.program_id(0)
    for live, a_ref, b_ref in (
        (step == 0, att_ref, g_att_ref),
        ((step > 0) & (step <= fold), n2_ref, g_hidden_ref),
        (step > fold, act_ref, g_mlp_ref),
    ):
        pl.when(live)(
            functools.partial(outer_body, images, blocks, 0, meta, a_ref, b_ref, out_ref, acc)
        )


def outer_block_call(sz, meta, att, g_branch, n2, g_hidden, act, g_mlp):
    w, fold = sz.width, sz.hidden // sz.width
    one = whole((sz.rows, w))

    def part(first):
        return pl.BlockSpec((sz.rows, w), lambda j, c: (0, jnp.clip(j - first, 0, fold - 1)))

    return pl.pallas_call(
        functools.partial(outer_block_body, sz.images, sz.blocks, fold),
        grid_spec=pltpu.PrefetchScalarGridSpec(
            num_scalar_prefetch=1,
            grid=(1 + 2 * fold,),
            in_specs=[one, one, one, part(1), part(1 + fold), one],
            out_specs=pl.BlockSpec((w, w), lambda j, c: (0, j)),
            scratch_shapes=[pltpu.VMEM((w, w), wide)],
        ),
        out_shape=jax.ShapeDtypeStruct((w, (1 + 2 * fold) * w), low),
        compiler_params=params(1),
        cost_estimate=cost(2 * sz.rows * w * w * (1 + 2 * fold), 2 * sz.rows * w * (2 * fold + 4)),
        name="grad_block",
    )(meta, att, g_branch, n2, g_hidden, act, g_mlp)


def outer_qkv_body(images, blocks, units, meta, n1_ref, dq_ref, dk_ref, dv_ref, out_ref, acc):
    for k, b_ref in enumerate((dq_ref, dk_ref, dv_ref)):
        pl.when(pl.program_id(0) == k)(
            functools.partial(outer_body, images, blocks, units, meta, n1_ref, b_ref, out_ref, acc)
        )


def outer_qkv_call(sz, meta, n1, dq, dk, dv, units):
    w = sz.width
    return pl.pallas_call(
        functools.partial(outer_qkv_body, sz.images, sz.blocks, units),
        grid_spec=pltpu.PrefetchScalarGridSpec(
            num_scalar_prefetch=1,
            grid=(3,),
            in_specs=[whole((sz.rows, w))] * 4,
            out_specs=pl.BlockSpec((units, w // units, w), lambda j, c: (0, 0, j)),
            scratch_shapes=[pltpu.VMEM((w, w), wide)],
        ),
        out_shape=jax.ShapeDtypeStruct((units, w // units, 3 * w), low),
        compiler_params=params(1),
        cost_estimate=cost(6 * sz.rows * w * w, 8 * sz.rows * w),
        name="grad_qkv",
    )(meta, n1, dq, dk, dv)


def place_body(at, kept, taken, out):
    i = pl.program_id(0)

    @pl.when(at[2 * i] == 1)
    def _():
        out[...] = kept[0]

    @pl.when(at[2 * i] == 0)
    def _():
        out[...] = taken[...].astype(wide)


def place_call(at, kept, taken, groups, rows):
    width = kept.shape[-1]
    spec = pl.BlockSpec((1, rows, width), lambda i, at: (at[2 * i + 1], 0, 0))
    kept_spec = pl.BlockSpec(
        (1, 1, rows, width), lambda i, at: (at[2 * i + 1], at[2 * groups], 0, 0)
    )
    return pl.pallas_call(
        place_body,
        grid_spec=pltpu.PrefetchScalarGridSpec(
            num_scalar_prefetch=1,
            grid=(groups,),
            in_specs=[kept_spec, spec],
            out_specs=pl.BlockSpec((1, rows, width), lambda i, at: (i, 0, 0)),
        ),
        out_shape=jax.ShapeDtypeStruct((groups, rows, width), wide),
        compiler_params=params(1),
        cost_estimate=cost(0, groups * rows * width * 10),
        name="place",
    )(at, kept, taken)


def attend_back_body(
    images, blocks, meta, q_ref, k_ref, v_ref, g_ref, lse_ref, delta_ref, dq_ref, dk_ref, dv_ref,
    dk_acc, dv_acc,
):
    at = pl.program_id(0)
    count, length = meta[at], meta[images + at]
    lane = lax.broadcasted_iota(jnp.int32, (BLOCK, PAIR), 1)
    first = lane < HEAD_DIM

    def keep(value, head):
        own = first if head == 0 else jnp.logical_not(first)
        zero = jnp.zeros_like(value[:BLOCK])
        return jnp.concatenate(
            [
                jnp.where(own, value[r : r + BLOCK], zero)
                for r in range(0, value.shape[0], BLOCK)
            ],
            axis=0,
        )

    def variant(keys_in):
        near = keys_in - BLOCK
        valid = lax.broadcasted_iota(jnp.int32, (BLOCK, BLOCK), 0) + near < length
        keys = k_ref[:keys_in, :]
        kept_keys = [keep(keys, head) for head in range(2)]
        values = v_ref[:keys_in, :]
        kept_values = [keep(values, head) for head in range(2)]
        dk_acc[:keys_in, :] = jnp.zeros((keys_in, PAIR), wide)
        dv_acc[:keys_in, :] = jnp.zeros((keys_in, PAIR), wide)

        @pl.loop(0, count)
        def _(step):
            rows = pl.ds(pl.multiple_of(step * BLOCK, BLOCK), BLOCK)
            q, g = q_ref[rows, :], g_ref[rows, :]
            dq = None
            for head in range(2):
                log = lse_ref[0, head : head + 1, rows]
                drop = delta_ref[0, head : head + 1, rows]
                score = dot_nt(kept_keys[head], q) * 0.125
                share = jnp.exp(score - log)
                if near:
                    share = jnp.concatenate(
                        [share[:near], jnp.where(valid, share[near:], 0.0)], axis=0
                    )
                else:
                    share = jnp.where(valid, share, 0.0)
                reach = dot_nt(kept_values[head], g)
                grad = (share * (reach - drop)).astype(low)
                dv_acc[:keys_in, :] += dot_nn(share.astype(low), keep(g, head))
                dk_acc[:keys_in, :] += dot_nn(grad, keep(q, head))
                term = dot_tn(grad, kept_keys[head])
                dq = term if dq is None else dq + term
            dq_ref[rows, :] = (dq * 0.125).astype(low)

        dk_ref[:keys_in, :] = (dk_acc[:keys_in, :] * 0.125).astype(low)
        dv_ref[:keys_in, :] = dv_acc[:keys_in, :].astype(low)

    for keys in range(1, blocks + 1):
        pl.when(count == keys)(functools.partial(variant, keys * BLOCK))


def attend_back_call(sz, meta, qkv, g_att, lse, delta):
    pairs = sz.pairs

    def spec(part):
        return pl.BlockSpec((sz.length, PAIR), lambda i, p, m: (i, part * pairs + p))

    line = pl.BlockSpec((1, 8, sz.length), lambda i, p, m: (i, p, 0))
    out = jax.ShapeDtypeStruct((sz.rows, sz.width), low)
    return pl.pallas_call(
        functools.partial(attend_back_body, sz.images, sz.blocks),
        grid_spec=pltpu.PrefetchScalarGridSpec(
            num_scalar_prefetch=1,
            grid=(sz.images, pairs),
            in_specs=[spec(0), spec(1), spec(2), spec(0), line, line],
            out_specs=[spec(0), spec(0), spec(0)],
            scratch_shapes=[pltpu.VMEM((sz.length, PAIR), wide)] * 2,
        ),
        out_shape=[out, out, out],
        compiler_params=params(2),
        cost_estimate=cost(
            10 * sz.rows * sz.length * sz.width,
            14 * sz.rows * sz.width,
            sz.rows * sz.length * HEADS,
        ),
        name="attend_back",
    )(meta, qkv, qkv, qkv, g_att, lse, delta)


def qkv_back_body(
    base, meta, x, g_res, dq, dk, dv, vec, mine, theirs, grad_ref, low_ref, sums, held, sems
):
    @pl.when(is_first())
    def _():
        fetch_all(meta, base, (mine, theirs), held, sems)
        sums[...] = jnp.zeros_like(sums)

    live = pl.program_id(1) < meta[pl.program_id(0)]

    @pl.when(live)
    def _():
        width = x.shape[1]
        normal, scale = normalise(x[...].astype(wide))
        back = None
        for part, ref in enumerate((dq, dk, dv)):
            term = dot_nt(ref[...], columns(held, part * width, width))
            back = term if back is None else back + term
        sums[0:1, :] += column_sum(back * normal)
        sums[1:2, :] += column_sum(back)
        sums[2:3, :] += column_sum(dq[...].astype(wide))
        sums[3:4, :] += column_sum(dv[...].astype(wide))
        grad = g_res[...] + norm_back(back, row_of(vec, NORM1_GAIN), normal, scale)
        grad_ref[...] = grad
        low_ref[...] = grad.astype(low)

    @pl.when(jnp.logical_not(live))
    def _():
        grad_ref[...] = jnp.zeros_like(grad_ref)
        low_ref[...] = jnp.zeros_like(low_ref)


def qkv_back_call(sz, meta, x, g_res, dq, dk, dv, vec, weight):
    w, blocks = sz.width, sz.blocks
    plain = pl.BlockSpec((BLOCK, w), lambda i, b, m: (i * blocks + b, 0))
    return pl.pallas_call(
        functools.partial(qkv_back_body, 2 * sz.images),
        grid_spec=pltpu.PrefetchScalarGridSpec(
            num_scalar_prefetch=1,
            grid=(sz.images, blocks),
            in_specs=[sz.row_spec(w)] * 5 + [whole(vec.shape), anywhere, anywhere],
            out_specs=[plain, plain, pl.BlockSpec((8, w), lambda i, b, m: (0, 0))],
            scratch_shapes=held_scratch(weight),
        ),
        out_shape=[
            jax.ShapeDtypeStruct((sz.rows, w), wide),
            jax.ShapeDtypeStruct((sz.rows, w), low),
            jax.ShapeDtypeStruct((8, w), wide),
        ],
        compiler_params=params(2),
        cost_estimate=cost(6 * sz.rows * w * w, sz.rows * w * 18 + 6 * w * w),
        name="qkv_back",
    )(meta, x, g_res, dq, dk, dv, vec, *weight)


axes = ("img", "seq")


def bits_of(count):
    return [1 << k for k in range(count.bit_length() - 1)]


def tied(value, *after):
    return lax.optimization_barrier((value, *after))[0]


def together(*values):
    return lax.optimization_barrier(values)


def cut(size, shares):
    edges = [round(size * sum(shares[:k]) / sum(shares) / 16) * 16 for k in range(len(shares) + 1)]
    return [slice(p, q) for p, q in zip(edges[:-1], edges[1:], strict=True)]


class Wires:
    def __init__(self, img_count, seq_count):
        self.count, self.seq_count = img_count * seq_count, seq_count
        self.core = seq_count
        self.units = img_count
        self.seq_bits = bits_of(seq_count)
        inner = [bit for bit in bits_of(self.count) if bit > self.core]
        inner = inner[:1] + inner[:0:-1]
        self.orders = (inner, inner[1:] + inner[:1])

    def swap(self, value, bit):
        return lax.ppermute(value, axes, [(i, i ^ bit) for i in range(self.count)])

    def step(self, value, at):
        pairs = [(i, i ^ self.orders[1 if i & self.core else 0][at]) for i in range(self.count)]
        return lax.ppermute(value, axes, pairs)

    def tables(self, me):
        img = me // self.seq_count
        core = img % 2

        def at(place, side):
            by_core = []
            for order in self.orders:
                unit = 0
                for k, bit in enumerate(order):
                    unit |= ((place >> k) & 1) * (bit // self.seq_count)
                by_core.append(unit)
            which = core if side == 0 else 1 - core
            return (img ^ side) ^ jnp.where(which == 0, by_core[0], by_core[1])

        def place(unit):
            side = (unit ^ img) & 1
            delta = unit ^ img
            by_core = []
            for order in self.orders:
                total = jnp.zeros((), jnp.int32)
                for k, bit in enumerate(order):
                    shift = (bit // self.seq_count).bit_length() - 1
                    total = total | (((delta >> shift) & 1) << k)
                by_core.append(total)
            which = core ^ side
            return side * (self.units // 2) + jnp.where(which == 0, by_core[0], by_core[1])

        half = self.units // 2
        order = [at(k, side) for side in range(2) for k in range(half)]
        inverse = [place(unit) for unit in range(self.units)]
        return jnp.stack(order + inverse)

    def join_seq(self, value, me):
        for bit in self.seq_bits:
            other = self.swap(value, bit)
            value = jnp.where(
                (me & bit) > 0,
                jnp.concatenate([other, value], axis=0),
                jnp.concatenate([value, other], axis=0),
            )
        return value

    def joined(self, value, at):
        return jnp.concatenate([value, self.step(value, at)], axis=0)

    def halved(self, value, at):
        half = value.shape[0] // 2
        return value[:half] + self.step(value[half:], at)

    def small_scatter(self, value, me, bits):
        for bit in reversed(bits):
            value = self.small_half(value, me, bit)
        return value[0]

    def small_half(self, value, me, bit):
        pair = value.reshape((2, value.shape[0] // 2) + value.shape[1:])
        up = (me & bit) > 0
        return jnp.where(up, pair[1], pair[0]) + self.swap(jnp.where(up, pair[0], pair[1]), bit)


def local(img_count, seq_count, *args):
    (
        patches, lengths, pooled_cot, norm1_gain, norm1_bias, qkv_weight, query_bias, value_bias,
        attn_weight, attn_bias, norm2_gain, norm2_bias, fc1_weight, fc1_bias, fc2_weight, fc2_bias,
        final_gain, final_bias, probe_vector, pool_query_weight, pool_query_bias, pool_kv_weight,
        pool_value_bias, pool_out_weight, pool_out_bias, head_gain, head_bias, head_fc1_weight,
        head_fc1_bias, head_fc2_weight, head_fc2_bias,
    ) = args
    count = img_count * seq_count
    groups, part_rows, width = patches.shape
    length = part_rows * seq_count
    hidden = fc1_weight.shape[1]
    images = max(1, groups // seq_count)
    share = max(1, seq_count // groups)
    own = width // count
    per = hidden // count
    fold = hidden // width
    sz = Sizes(images, length, width, hidden)
    wires = Wires(img_count, seq_count)
    me = lax.axis_index(axes)
    seq_at = lax.axis_index("seq")
    first_image = (seq_at // share) * images

    slots = list(range(groups))
    if share == 1:
        turn = [r % seq_count if (r // seq_count) % 2 == 0 else -1 - r % seq_count for r in slots]
        slots = [(t % seq_count) * images + r // seq_count for r, t in zip(slots, turn, strict=True)]
        ahead = (lengths[None, :] > lengths[:, None]) | (
            (lengths[None, :] == lengths[:, None])
            & (jnp.arange(groups)[None, :] < jnp.arange(groups)[:, None])
        )
        rank = jnp.sum(ahead, axis=1)
        slot_of = sum(jnp.where(rank == r, slot, 0) for r, slot in enumerate(slots))
    else:
        slot_of = jnp.arange(groups)
    order = jnp.sum(
        jnp.where(slot_of[None, :] == jnp.arange(groups)[:, None], jnp.arange(groups)[None, :], 0),
        axis=1,
    )

    def of_slots(value, first):
        at = lax.dynamic_slice_in_dim(order, first, images)
        return jnp.concatenate(
            [lax.dynamic_slice_in_dim(value, at[k], 1) for k in range(images)], axis=0
        )

    own_lengths = of_slots(lengths, first_image)
    own_lengths = jnp.where(seq_at % share == 0, own_lengths, 0)
    own_cot = of_slots(pooled_cot, first_image)
    meta = jnp.concatenate(
        [(own_lengths + BLOCK - 1) // BLOCK, own_lengths, wires.tables(me)]
    ).astype(jnp.int32)

    def by_unit(bias):
        return bias.reshape(own, fold).T

    vectors = [
        v.reshape(1, own)
        for v in (
            norm1_gain, norm1_bias, query_bias, value_bias, attn_bias, norm2_gain, norm2_bias,
            fc2_bias, final_gain, final_bias, pool_query_bias, pool_value_bias, pool_out_bias,
            head_gain, head_bias, head_fc2_bias, probe_vector,
        )
    ]
    vectors += [by_unit(fc1_bias), by_unit(head_fc1_bias)]
    unit_a, block, pack = packs_call(
        vectors, qkv_weight, pool_kv_weight, pool_query_weight, attn_weight, fc1_weight, fc2_weight,
        pool_out_weight, head_fc1_weight, head_fc2_weight,
    )
    block = lax.all_gather(block, axes, axis=0, tiled=True)

    pairwise = seq_count == 2 and share == 1
    steps = len(wires.orders[0])
    if pairwise:
        kept = of_slots(patches, first_image)
        given = of_slots(patches, (1 - seq_at) * images)
        parts = cut(part_rows, list(range(2, steps + 2)))
    else:
        ordered = jnp.concatenate(
            [lax.dynamic_slice_in_dim(patches, order[k], 1) for k in range(groups)], axis=0
        )
        given = jnp.repeat(ordered, share, axis=0)
    mine = wires.join_seq(unit_a, me)[None]
    mine, given = together(mine, given)
    taken = []
    for at in range(steps):
        mine = wires.joined(mine, at)
        if pairwise:
            mine, one = together(mine, wires.swap(given[:, parts[at]], 1))
            taken.append(one)
        if at == 1:
            mine, meta = together(mine, meta)
    mine, pack = together(mine, pack)
    theirs = wires.swap(mine, wires.core)
    theirs, pack = together(theirs, pack)
    qkv_full = (mine, theirs)
    if pairwise:
        taken = jnp.concatenate(taken, axis=1)
        x = jnp.where(
            seq_at == 0,
            jnp.concatenate([kept, taken], axis=1),
            jnp.concatenate([taken, kept], axis=1),
        )
    else:
        x = lax.all_to_all(given, "seq", split_axis=0, concat_axis=1, tiled=True)
    x = x.reshape(sz.rows, width)

    qkv, n1, vec = qkv_call(sz, meta, x, qkv_full)
    pack = wires.join_seq(pack, me)[None]
    qkv, pack = together(qkv, pack)
    done, forward = 0, ()
    for at in range(images):
        forward = attend_call(sz, meta, qkv, at, forward)
        stop = steps - 1 if at == images - 1 else min(done + 1, steps - 1)
        while done < stop:
            pack = wires.joined(pack, done)
            done += 1
        *forward, pack = together(*forward, pack)
    att, lse = forward
    res, n2, slope, act, enc, fin = mlp_call(sz, meta, x, att, vec, block)
    other = wires.swap(pack, wires.core)
    pack_rest = wires.step(pack, steps - 1)
    fin, other, pack_rest = together(fin, other, pack_rest)
    other_rest = wires.swap(pack_rest, wires.core)
    head_full = (jnp.concatenate([pack, pack_rest], axis=0), other, other_rest)
    cot_rows = jnp.pad(own_cot, ((0, HEAD_ROWS - images), (0, 0)))
    shares, g_score, lift, probe_w, sent, head_sums = head_call(
        sz, meta, fin, cot_rows, vec, block, head_full
    )
    rows = lax.all_gather(sent, axes, axis=0, tiled=True)

    g_mlp, g_hidden, g_res, g_branch, g_att, delta, back_sums = back_call(
        sz, meta, fin, enc, res, att, slope, g_score, shares, lift, probe_w, vec, block
    )
    terms = outer_block_call(sz, meta, att, g_branch, n2, g_hidden, act, g_mlp)
    terms, g_att, rows = together(terms, g_att, rows)
    totals = lax.psum_scatter(terms, axes, scatter_dimension=0, tiled=True)

    def by_column(grad):
        return grad.reshape(own, fold, width).transpose(0, 2, 1).reshape(own, hidden)

    def own_part(v, axis=-1):
        return lax.dynamic_slice_in_dim(v, me * own, own, axis=axis)

    half = wires.units // 2
    dq, dk, dv = attend_back_call(sz, meta, qkv, g_att, lse, delta)
    last = outer_qkv_call(sz, meta, n1, dq, dk, dv, wires.units)
    g_res, last = together(g_res, last)
    last = last[:half] + wires.swap(last[half:], wires.core)
    patch_grad, patch_low, qkv_sums = qkv_back_call(sz, meta, x, g_res, dq, dk, dv, vec, qkv_full)
    patch_low = patch_low.reshape(images, length, width)
    sums = jnp.concatenate(
        [back_sums[:6], head_sums[:2], qkv_sums[:4], back_sums[8 : 8 + fold]], axis=0
    )
    sums = sums.reshape(-1, count, own).transpose(1, 0, 2)
    if pairwise:
        given = lax.dynamic_slice_in_dim(patch_low, (1 - seq_at) * part_rows, part_rows, axis=1)
    else:
        given = lax.all_to_all(patch_low, "seq", split_axis=1, concat_axis=0, tiled=True)[::share]

    def head_part(rows):
        narrow = own_part(rows.reshape(count * images, SENT_ROWS, width))
        rows = rows.reshape(count * images, SENT_ROWS, width)
        act_own = narrow[:, SENT_ACT : SENT_ACT + fold].transpose(0, 2, 1).reshape(-1, per)
        grad_pool_v = jnp.einsum(
            "ihr,ihd->rhd",
            narrow[:, :HEADS],
            rows[:, SENT_PULL].reshape(-1, HEADS, HEAD_DIM),
            preferred_element_type=wide,
        ).reshape(own, width)
        return (
            dot_tn(act_own, rows[:, SENT_COT]),
            dot_tn(narrow[:, SENT_POOLED], rows[:, SENT_BRANCH]),
            grad_pool_v,
            narrow[:, SENT_NORMED],
            jnp.sum(narrow[:, SENT_MIX : SENT_MIX + HEADS].astype(wide), axis=0),
        )

    def hidden_part(rows, normed_own):
        rows = rows.reshape(count * images, SENT_ROWS, width)
        head_grad = rows[:, SENT_GRAD : SENT_GRAD + fold].reshape(count * images, hidden)
        return by_column(dot_tn(normed_own, head_grad))

    def sums_part(rows, mix_own):
        rows = rows.reshape(count * images, SENT_ROWS, width)
        row_sums = jnp.sum(rows[:, 2 * HEAD_ROWS - 1 :].astype(wide), axis=0)
        query_grad = row_sums[SENT_QUERY - 2 * HEAD_ROWS + 1] + row_sums[0]
        pool_query = probe_w[HEADS]
        grad_pool_k = (
            0.125 * mix_own.T[:, :, None] * pool_query.reshape(1, HEADS, HEAD_DIM)
        ).reshape(own, width)
        pooled = rows[:, SENT_OUT].astype(wide) + rows[:, SENT_OUT_REST].astype(wide)
        pooled = pooled.reshape(img_count, seq_count, images, width)[:, ::share]
        pooled = lax.dynamic_index_in_dim(pooled, me // seq_count, 0, keepdims=False)
        pooled = pooled.reshape(groups, width)
        pooled = jnp.concatenate(
            [lax.dynamic_slice_in_dim(pooled, slot_of[k], 1) for k in range(groups)], axis=0
        )
        return (
            pooled,
            probe_vector.astype(wide)[:, None] * query_grad[None, :],
            jnp.sum(pool_query_weight.astype(wide) * query_grad[None, :], axis=1),
            grad_pool_k,
            own_part(query_grad),
            own_part(row_sums),
        )

    last, sums, given, rows = together(last, sums, given, rows)
    parts, taken, made = cut(part_rows, (1,) * steps), [], []
    bits = list(reversed(bits_of(count)))
    for tick, at in enumerate(reversed(range(steps))):
        last = wires.halved(last, at)
        sums = wires.small_half(sums, me, bits.pop(0))
        taken.append(wires.swap(given[:, parts[tick]], 1) if pairwise else given)
        if tick == 0:
            made.append(head_part(rows))
        elif tick == 1:
            made.append(hidden_part(rows, made[0][3]))
        elif tick == 2:
            made.append(sums_part(rows, made[0][4]))
        last, sums, rows, taken, made = together(last, sums, rows, taken, made)
    (grad_head_fc2, grad_pool_out, grad_pool_v, _, _), grad_head_fc1, made = made
    pooled, grad_pool_query_weight, grad_probe, grad_pool_k, g_pool_query_bias, own_sums = made
    grad_pool_kv = jnp.concatenate([grad_pool_k, grad_pool_v], axis=1)

    def own_sum(at):
        return own_sums[at - 2 * HEAD_ROWS + 1]

    g_head_fc1_bias = own_sums[SENT_GRAD - 2 * HEAD_ROWS + 1 :][:fold].T.reshape(per)
    last = last.reshape(seq_count, own, 3 * width)
    for bit in reversed(wires.seq_bits):
        last = wires.small_half(last, me, bit)
    while bits:
        sums = wires.small_half(sums, me, bits.pop(0))
    if pairwise:
        at_slot = jnp.stack(
            [(slot_of // images == seq_at).astype(jnp.int32), slot_of % images], axis=1
        )
        at_slot = jnp.concatenate([at_slot.reshape(-1), seq_at[None]]).astype(jnp.int32)
        patch_grad = place_call(
            at_slot,
            patch_grad.reshape(images, seq_count, part_rows, width),
            jnp.concatenate(taken, axis=1),
            groups,
            part_rows,
        )
    else:
        patch_grad = jnp.concatenate(
            [lax.dynamic_slice_in_dim(taken[0], slot_of[k], 1) for k in range(groups)], axis=0
        ).astype(wide)
    totals = totals.astype(wide)
    grad_attn = totals[:, :width]
    grad_fc1 = by_column(totals[:, width : width + hidden])
    grad_fc2 = totals[:, width + hidden :].reshape(per, width)
    grad_qkv = last[0].astype(wide)
    sums = sums[0]
    (
        g_final_gain, g_final_bias, g_fc2_bias, g_norm2_gain, g_norm2_bias, g_attn_bias,
        g_head_gain, g_head_bias, g_norm1_gain, g_norm1_bias, g_query_bias, g_value_bias,
    ) = sums[:12]
    g_fc1_bias = sums[12:].T.reshape(per)
    return (
        pooled, patch_grad, g_norm1_gain, g_norm1_bias, grad_qkv, g_query_bias, g_value_bias,
        grad_attn, g_attn_bias, g_norm2_gain, g_norm2_bias, grad_fc1, g_fc1_bias, grad_fc2,
        g_fc2_bias, g_final_gain, g_final_bias, grad_probe, grad_pool_query_weight,
        g_pool_query_bias, grad_pool_kv, own_sum(SENT_PULL), grad_pool_out,
        own_sum(SENT_BRANCH), g_head_gain, g_head_bias, grad_head_fc1,
        g_head_fc1_bias, grad_head_fc2, own_sum(SENT_COT),
    )


def solution(mesh):
    rows, vector = P(axes, None), P(axes)
    body = functools.partial(local, mesh.shape["img"], mesh.shape["seq"])
    vector_weights = (3, 4, 6, 7, 9, 10, 11, 13, 15, 16, 17, 18, 20, 22, 24, 25, 26, 28, 30)
    in_specs = (P("img", "seq", None), P("img"), P("img", None)) + tuple(
        vector if at in vector_weights else rows for at in range(3, 31)
    )
    out_specs = (P("img", None), P("img", "seq", None)) + in_specs[3:]
    return jax.shard_map(body, mesh=mesh, in_specs=in_specs, out_specs=out_specs, check_vma=False)
```

profile of v0, /device:TPU:0, one launch (start us, length us, event | category | flops | bytes accessed | tf_op | source)
XLA Modules:
  0.0 527.0 jit_solution(6108022645274750222)
XLA Ops:
  10.1 3.6 packs.1
  13.8 3.0 collective-permute-start
  31.7 3.8 collective-permute-done.1
  36.3 5.2 collective-permute-done.2
  47.0 16.8 %collective-permute-done.3 = bf16[2,48,2432]{2,1,0:T(8,128)(2,1)} collective-permute-done((bf16[2,48,2432]{2,1,0:T(8,128)(2,1)}, bf16[2,48,2432]{2,1,0:T(8,128)(2,1)}, u32[]{:S(2)}, u32[]{:S(2)}) %collective-permute-start.3) | collective-permute-done | bytes 466976 | tf_op jit(solution)/shard_map/ppermute | solution.py:987
  65.1 3.1 collective-permute-start.5
  68.4 19.3 %collective-permute-done.5 = bf16[4,48,2432]{2,1,0:T(8,128)(2,1)S(1)} collective-permute-done((bf16[4,48,2432]{2,1,0:T(8,128)(2,1)S(1)}, bf16[4,48,2432]{2,1,0:T(8,128)(2,1)S(1)}, u32[]{:S(2)}, u32[]{:S(2)}) %collective-permute-start.5) | collective-permute-done | bytes 933920 | tf_op jit(solution)/shard_map/ppermute | solution.py:987
  89.2 2.8 collective-permute-start.7
  91.9 4.1 maximum_select_fusion
  96.1 6.6 %collective-permute-start.8 = (bf16[24,6144]{1,0:T(8,128)(2,1)S(1)}, bf16[24,6144]{1,0:T(8,128)(2,1)S(1)}, u32[]{:S(2)}, u32[]{:S(2)}) collective-permute-start(bf16[24,6144]{1,0:T(8,128)(2,1)S(1)} %copy-done.3), channel_id=1, source_target_pairs={{0,1},{1,0},{2,3},{3,2},{4,5},{5,4},{6,7},{7,6},{8,9},{9,8},{10,11... | collective-permute-start | bytes 884744 | tf_op jit(solution)/shard_map/ppermute | solution.py:983
  102.6 13.4 %qkv.1 = (bf16[2048,2304]{1,0:T(8,128)(2,1)}, bf16[2048,768]{1,0:T(8,128)(2,1)}, f32[32,768]{1,0:T(8,128)}) custom-call(s32[36]{0:T(128)} %concatenate.114.meta, bf16[2048,768]{1,0:T(8,128)(2,1)} %bitcast.175, bf16[8,48,2432]{2,1,0:T(8,128)(2,1)} %pad_maximum_fusion.2.mine, bf16[8,48,2432]{2,1,0:T(8,128)(2,1)} %collective-permute-done.7.theirs), custom_call_target="tpu_custom_call" | custom-call | flops 7247757312 | bytes 19267584 | tf_op jit(solution)/shard_map/qkv/pallas_call | solution.py:250
  116.7 2.6 collective-permute-start.9
  119.3 20.9 %attend_0.1 = (bf16[2048,768]{1,0:T(8,128)(2,1)}, f32[2,48,1024]{2,1,0:T(8,128)}) custom-call(s32[36]{0:T(128)} %concatenate.114.meta, bf16[2048,2304]{1,0:T(8,128)(2,1)} %get-tuple-element.150.q_ref.k_ref.v_ref, bf16[2048,2304]{1,0:T(8,128)(2,1)} %get-tuple-element.150.q_ref.k_ref.v_ref, bf16[2048,2304]{1,0:T(8,128)(2,1)} %get-tuple-element.150.q_ref.k_ref.v_ref), custom_call_target="tpu_custom_call" | custom-call | flops 3221225472 | bytes 6291456 | tf_op jit(solution)/shard_map/attend_0/pallas_call | solution.py:321
  140.4 12.4 %attend_1.1 = (bf16[2048,768]{1,0:T(8,128)(2,1)}, f32[2,48,1024]{2,1,0:T(8,128)}) custom-call(s32[36]{0:T(128)} %concatenate.114.meta, bf16[2048,2304]{1,0:T(8,128)(2,1)} %get-tuple-element.150.q_ref.k_ref.v_ref, bf16[2048,2304]{1,0:T(8,128)(2,1)} %get-tuple-element.150.q_ref.k_ref.v_ref, ...), custom_call_target="tpu_custom_call", output_to_operand_aliasing={{0}: (4, {}), {1}: (5, {})} | custom-call | flops 3221225472 | bytes 6291456 | tf_op jit(solution)/shard_map/attend_1/pallas_call | solution.py:321
  152.9 16.4 %collective-permute-done.10 = bf16[2,48,6144]{2,1,0:T(8,128)(2,1)} collective-permute-done((bf16[2,48,6144]{2,1,0:T(8,128)(2,1)S(1)}, bf16[2,48,6144]{2,1,0:T(8,128)(2,1)}, u32[]{:S(2)}, u32[]{:S(2)}) %collective-permute-start.10) | collective-permute-done | bytes 1179680 | tf_op jit(solution)/shard_map/ppermute | solution.py:987
  170.7 2.6 collective-permute-start.11
  175.0 34.4 %mlp.1 = (f32[2048,768]{1,0:T(8,128)}, bf16[2048,768]{1,0:T(8,128)(2,1)}, bf16[2048,3072]{1,0:T(8,128)(2,1)}, bf16[2048,3072]{1,0:T(8,128)(2,1)}, f32[2048,768]{1,0:T(8,128)}, /*index=5*/bf16[2048,768]{1,0:T(8,128)(2,1)}) custom-call(s32[36]{0:T(128)} %concatenate.114.meta, bf16[2048,768]{1,0:T(8,128)(2,1)} %bitcast.176, ...), custom_call_target="tpu_custom_call" | custom-call | flops 21743271936 | bytes 56623104 | tf_op jit(solution)/shard_map/mlp/pallas_call | solution.py:386
  209.5 11.6 %collective-permute-start.13 = (bf16[4,48,6144]{2,1,0:T(8,128)(2,1)}, bf16[4,48,6144]{2,1,0:T(8,128)(2,1)}, u32[]{:S(2)}, u32[]{:S(2)}) collective-permute-start(bf16[4,48,6144]{2,1,0:T(8,128)(2,1)} %collective-permute-done.12), channel_id=1, source_target_pairs={{0,2},{1,3},{2,0},{3,1},{4,6},{5,7},{6,4},{7,5},{8,10},{9,11},{10,... | collective-permute-start | bytes 7077896 | tf_op jit(solution)/shard_map/ppermute | solution.py:983
  221.7 4.2 pad_maximum_fusion.mine
  225.9 24.8 %head.1 = (f32[2,16,1024]{2,1,0:T(8,128)}, f32[2,16,1024]{2,1,0:T(8,128)}, f32[2,16,768]{2,1,0:T(8,128)}, f32[16,768]{1,0:T(8,128)}, bf16[96,768]{1,0:T(8,128)(2,1)}, /*index=5*/f32[8,768]{1,0:T(8,128)}) custom-call(s32[36]{0:T(128)} %concatenate.114.meta, bf16[2048,768]{1,0:T(8,128)(2,1)} %get-tuple-element.164.fin, f32[16,768]{1,0:T(8,128)} %select_maximum_fusion.cot_ref, ...), custom_call_target="tpu_custom_call" | custom-call | flops 301989888 | bytes 17301504 | tf_op jit(solution)/shard_map/head/pallas_call | solution.py:563
  251.6 37.6 %mlp_back.1 = (bf16[2048,768]{1,0:T(8,128)(2,1)}, bf16[2048,3072]{1,0:T(8,128)(2,1)}, f32[2048,768]{1,0:T(8,128)}, bf16[2048,768]{1,0:T(8,128)(2,1)}, bf16[2048,...) custom-call(s32[36]{0:T(128)} %concatenate.114.meta, bf16[2048,768]{1,0:T(8,128)(2,1)} %get-tuple-element.164.fin, ...), custom_call_target="tpu_custom_call" | custom-call | flops 21743271936 | bytes 69206016 | tf_op jit(solution)/shard_map/mlp_back/pallas_call | solution.py:656
  289.2 28.6 %grad_block.1 = bf16[768,6912]{1,0:T(8,128)(2,1)} custom-call(s32[36]{0:T(128)} %concatenate.114.meta, bf16[2048,768]{1,0:T(8,128)(2,1)} %get-tuple-element.159.att.att_ref, bf16[2048,768]{1,0:T(8,128)(2,1)} %get-tuple-element.176.g_att_ref, bf16[2048,768]{1,0:T(8,128)(2,1)} %get-tuple-element.177.n2_ref, ...), custom_call_target="tpu_custom_call" | custom-call | flops 21743271936 | bytes 37748736 | tf_op jit(solution)/shard_map/grad_block/pallas_call | solution.py:734
  319.0 38.9 %attend_back.1 = (bf16[2048,768]{1,0:T(8,128)(2,1)}, bf16[2048,768]{1,0:T(8,128)(2,1)}, bf16[2048,768]{1,0:T(8,128)(2,1)}) custom-call(s32[36]{0:T(128)} %concatenate.114.meta, bf16[2048,2304]{1,0:T(8,128)(2,1)} %get-tuple-element.150.q_ref.k_ref.v_ref, bf16[2048,2304]{1,0:T(8,128)(2,1)} %get-tuple-element.150.q_ref.k_ref.v_ref, ...), custom_call_target="tpu_custom_call" | custom-call | flops 16106127360 | bytes 22020096 | tf_op jit(solution)/shard_map/attend_back/pallas_call | solution.py:877
  357.9 13.5 %grad_qkv.1 = bf16[16,48,2304]{2,1,0:T(8,128)(2,1)} custom-call(s32[36]{0:T(128)} %concatenate.114.meta, bf16[2048,768]{1,0:T(8,128)(2,1)} %get-tuple-element.175.n1_ref, bf16[2048,768]{1,0:T(8,128)(2,1)} %get-tuple-element.186.dq_ref.dq, bf16[2048,768]{1,0:T(8,128)(2,1)} %get-tuple-element.187.dk_ref.dk, bf16[2048,768]{1,0:T(8,128)(2,1)} %get-tuple-element.188.dv_ref.dv), custom_call_target="tpu_custom_call" | custom-call | flops 7247757312 | bytes 12582912 | tf_op jit(solution)/shard_map/grad_qkv/pallas_call | solution.py:759
  384.1 17.8 %qkv_back.1 = (f32[2048,768]{1,0:T(8,128)}, bf16[2048,768]{1,0:T(8,128)(2,1)}, f32[8,768]{1,0:T(8,128)}) custom-call(s32[36]{0:T(128)} %concatenate.114.meta, bf16[2048,768]{1,0:T(8,128)(2,1)} %bitcast.177, f32[2048,768]{1,0:T(8,128)} %get-tuple-element.192.g_res, bf16[2048,768]{1,0:T(8,128)(2,1)} %get-tuple-element.186.dq_ref.dq, ...), custom_call_target="tpu_custom_call" | custom-call | flops 7247757312 | bytes 31850496 | tf_op jit(solution)/shard_map/qkv_back/pallas_call | solution.py:932
  407.3 3.3 slice_reduce_fusion
  419.5 23.9 %collective-permute-start.15 = (bf16[4,48,2304]{2,1,0:T(8,128)(2,1)}, bf16[4,48,2304]{2,1,0:T(8,128)(2,1)}, u32[]{:S(2)}, u32[]{:S(2)}) collective-permute-start(bf16[4,48,2304]{2,1,0:T(8,128)(2,1)} %slice.256), channel_id=1, source_target_pairs={{0,8},{1,9},{2,6},{3,7},{4,12},{5,13},{6,2},{7,3},{8,0},{9,1},{10,... | collective-permute-start | bytes 2654216 | tf_op jit(solution)/shard_map/ppermute | solution.py:987
  448.2 3.3 collective-permute-start.17
  458.3 3.2 collective-permute-done.16
  472.7 3.1 collective-permute-done.19
  475.9 10.8 %collective-permute-done.18 = bf16[2,48,2304]{2,1,0:T(8,128)(2,1)} collective-permute-done((bf16[2,48,2304]{2,1,0:T(8,128)(2,1)}, bf16[2,48,2304]{2,1,0:T(8,128)(2,1)}, u32[]{:S(2)}, u32[]{:S(2)}) %collective-permute-start.18) | collective-permute-done | bytes 442400 | tf_op jit(solution)/shard_map/ppermute | solution.py:987
  506.0 6.9 %place.1 = f32[4,512,768]{2,1,0:T(8,128)} custom-call(s32[9]{0:T(128)} %pad_add_fusion.1.at, f32[2,2,512,768]{3,2,1,0:T(8,128)} %bitcast.165, bf16[2,512,768]{2,1,0:T(8,128)(2,1)} %pad_maximum_fusion.4.taken), custom_call_target="tpu_custom_call" | custom-call | bytes 15728640 | tf_op jit(solution)/shard_map/place/pallas_call | solution.py:793
  (188 shorter events, 94.0 us)
Async XLA Ops:
  7.2 167.8 %all-gather.3.cloned.1.call-start = ((), (), s32[]{:S(2)}) async-start(), calls=%async_computation.1 | async-start | bytes 15814656 | tf_op jit(solution)/shard_map/all_gather | solution.py:1118
  13.8 305.2 %all-gather.5.cloned.1.call-start = ((), (), s32[]{:S(2)}) async-start(), calls=%async_computation.2 | async-start | bytes 4866048 | tf_op jit(solution)/shard_map/all_gather | solution.py:1178
  13.8 14.8 %collective-permute-start = (bf16[24,2432]{1,0:T(8,128)(2,1)}, bf16[24,2432]{1,0:T(8,128)(2,1)S(1)}, u32[]{:S(2)}, u32[]{:S(2)}) collective-permute-start(bf16[24,2432]{1,0:T(8,128)(2,1)} %get-tuple-element.133), channel_id=1, source_target_pairs={{0,1},{1,0},{2,3},{3,2},{4,5},{5,4},{6,7},{7,6},{8,9},{9,8},{10,11... | collective-permute-start | bytes 350216 | tf_op jit(solution)/shard_map/ppermute | solution.py:983
  29.4 6.1 %collective-permute-start.1 = (bf16[1,48,2432]{2,1,0:T(8,128)(2,1)S(1)}, bf16[1,48,2432]{2,1,0:T(8,128)(2,1)S(1)}, u32[]{:S(2)}, u32[]{:S(2)}) collective-permute-start(bf16[1,48,2432]{2,1,0:T(8,128)(2,1)S(1)} %maximum_select_fusion.2), channel_id=1, source_target_pairs={{0,4},{1,5},{2,18},{3,19},{4,0},{5,1},{6,22},{7,23},{8,12},{9,13},... | collective-permute-start | bytes 700424 | tf_op jit(solution)/shard_map/ppermute | solution.py:987
  31.0 10.5 %collective-permute-start.2 = (bf16[2,112,768]{2,1,0:T(8,128)(2,1)S(1)}, bf16[2,112,768]{2,1,0:T(8,128)(2,1)S(1)}, u32[]{:S(2)}, u32[]{:S(2)}) collective-permute-start(bf16[2,112,768]{2,1,0:T(8,128)(2,1)S(1)} %slice.244), channel_id=1, source_target_pairs={{0,1},{1,0},{2,3},{3,2},{4,5},{5,4},{6,7},{7,6},{8,9},{9,8},{10,11... | collective-permute-start | bytes 1032200 | tf_op jit(solution)/shard_map/ppermute | solution.py:983
  41.5 22.4 %collective-permute-start.3 = (bf16[2,48,2432]{2,1,0:T(8,128)(2,1)}, bf16[2,48,2432]{2,1,0:T(8,128)(2,1)}, u32[]{:S(2)}, u32[]{:S(2)}) collective-permute-start(bf16[2,48,2432]{2,1,0:T(8,128)(2,1)} %pad_maximum_fusion.7), channel_id=1, source_target_pairs={{0,16},{1,17},{2,10},{3,11},{4,20},{5,21},{6,14},{7,15},{8,24},{9,... | collective-permute-start | bytes 1400840 | tf_op jit(solution)/shard_map/ppermute | solution.py:987
  42.6 22.5 %collective-permute-start.4 = (bf16[2,176,768]{2,1,0:T(8,128)(2,1)}, bf16[2,176,768]{2,1,0:T(8,128)(2,1)}, u32[]{:S(2)}, u32[]{:S(2)}) collective-permute-start(bf16[2,176,768]{2,1,0:T(8,128)(2,1)} %slice.245), channel_id=1, source_target_pairs={{0,1},{1,0},{2,3},{3,2},{4,5},{5,4},{6,7},{7,6},{8,9},{9,8},{10,11... | collective-permute-start | bytes 1622024 | tf_op jit(solution)/shard_map/ppermute | solution.py:983
  65.1 22.6 %collective-permute-start.5 = (bf16[4,48,2432]{2,1,0:T(8,128)(2,1)S(1)}, bf16[4,48,2432]{2,1,0:T(8,128)(2,1)S(1)}, u32[]{:S(2)}, u32[]{:S(2)}) collective-permute-start(bf16[4,48,2432]{2,1,0:T(8,128)(2,1)S(1)} %pad_maximum_fusion.6), channel_id=1, source_target_pairs={{0,8},{1,9},{2,6},{3,7},{4,12},{5,13},{6,2},{7,3},{8,0},{9,1},{10,... | collective-permute-start | bytes 2801672 | tf_op jit(solution)/shard_map/ppermute | solution.py:987
  68.3 20.9 %collective-permute-start.6 = (bf16[2,224,768]{2,1,0:T(8,128)(2,1)S(1)}, bf16[2,224,768]{2,1,0:T(8,128)(2,1)S(1)}, u32[]{:S(2)}, u32[]{:S(2)}) collective-permute-start(bf16[2,224,768]{2,1,0:T(8,128)(2,1)S(1)} %slice.248), channel_id=1, source_target_pairs={{0,1},{1,0},{2,3},{3,2},{4,5},{5,4},{6,7},{7,6},{8,9},{9,8},{10,11... | collective-permute-start | bytes 2064392 | tf_op jit(solution)/shard_map/ppermute | solution.py:983
  89.2 6.9 %collective-permute-start.7 = (bf16[8,48,2432]{2,1,0:T(8,128)(2,1)}, bf16[8,48,2432]{2,1,0:T(8,128)(2,1)}, u32[]{:S(2)}, u32[]{:S(2)}) collective-permute-start(bf16[8,48,2432]{2,1,0:T(8,128)(2,1)} %pad_maximum_fusion.2.mine), channel_id=1, source_target_pairs={{0,2},{1,3},{2,0},{3,1},{4,6},{5,7},{6,4},{7,5},{8,10},{9,11},{10,... | collective-permute-start | bytes 5603336 | tf_op jit(solution)/shard_map/ppermute | solution.py:983
  96.1 20.5 %collective-permute-start.8 = (bf16[24,6144]{1,0:T(8,128)(2,1)S(1)}, bf16[24,6144]{1,0:T(8,128)(2,1)S(1)}, u32[]{:S(2)}, u32[]{:S(2)}) collective-permute-start(bf16[24,6144]{1,0:T(8,128)(2,1)S(1)} %copy-done.3), channel_id=1, source_target_pairs={{0,1},{1,0},{2,3},{3,2},{4,5},{5,4},{6,7},{7,6},{8,9},{9,8},{10,11... | collective-permute-start | bytes 884744 | tf_op jit(solution)/shard_map/ppermute | solution.py:983
  116.7 23.6 %collective-permute-start.9 = (bf16[1,48,6144]{2,1,0:T(8,128)(2,1)S(1)}, bf16[1,48,6144]{2,1,0:T(8,128)(2,1)S(1)}, u32[]{:S(2)}, u32[]{:S(2)}) collective-permute-start(bf16[1,48,6144]{2,1,0:T(8,128)(2,1)S(1)} %maximum_select_fusion.1), channel_id=1, source_target_pairs={{0,4},{1,5},{2,18},{3,19},{4,0},{5,1},{6,22},{7,23},{8,12},{9,13},... | collective-permute-start | bytes 1769480 | tf_op jit(solution)/shard_map/ppermute | solution.py:987
  140.4 28.9 %collective-permute-start.10 = (bf16[2,48,6144]{2,1,0:T(8,128)(2,1)S(1)}, bf16[2,48,6144]{2,1,0:T(8,128)(2,1)}, u32[]{:S(2)}, u32[]{:S(2)}) collective-permute-start(bf16[2,48,6144]{2,1,0:T(8,128)(2,1)S(1)} %pad_maximum_fusion.5), channel_id=1, source_target_pairs={{0,16},{1,17},{2,10},{3,11},{4,20},{5,21},{6,14},{7,15},{8,24},{9,... | collective-permute-start | bytes 3538952 | tf_op jit(solution)/shard_map/ppermute | solution.py:987
  170.7 38.7 %collective-permute-start.11 = (bf16[4,48,6144]{2,1,0:T(8,128)(2,1)S(1)}, bf16[4,48,6144]{2,1,0:T(8,128)(2,1)}, u32[]{:S(2)}, u32[]{:S(2)}) collective-permute-start(bf16[4,48,6144]{2,1,0:T(8,128)(2,1)S(1)} %pad_maximum_fusion.1), channel_id=1, source_target_pairs={{0,2},{1,3},{2,0},{3,1},{4,6},{5,7},{6,4},{7,5},{8,10},{9,11},{10,... | collective-permute-start | bytes 7077896 | tf_op jit(solution)/shard_map/ppermute | solution.py:983
  173.4 36.1 %collective-permute-start.12 = (bf16[4,48,6144]{2,1,0:T(8,128)(2,1)S(1)}, bf16[4,48,6144]{2,1,0:T(8,128)(2,1)}, u32[]{:S(2)}, u32[]{:S(2)}) collective-permute-start(bf16[4,48,6144]{2,1,0:T(8,128)(2,1)S(1)} %pad_maximum_fusion.1), channel_id=1, source_target_pairs={{0,8},{1,9},{2,6},{3,7},{4,12},{5,13},{6,2},{7,3},{8,0},{9,1},{10,... | collective-permute-start | bytes 7077896 | tf_op jit(solution)/shard_map/ppermute | solution.py:987
  175.0 46.0 %copy-start.8 = (f32[4,768]{1,0:T(4,128)S(1)}, f32[4,768]{1,0:T(4,128)}, u32[]{:S(2)}) copy-start(f32[4,768]{1,0:T(4,128)} %param.33) | copy-start | bytes 36868
  209.5 16.4 %collective-permute-start.13 = (bf16[4,48,6144]{2,1,0:T(8,128)(2,1)}, bf16[4,48,6144]{2,1,0:T(8,128)(2,1)}, u32[]{:S(2)}, u32[]{:S(2)}) collective-permute-start(bf16[4,48,6144]{2,1,0:T(8,128)(2,1)} %collective-permute-done.12), channel_id=1, source_target_pairs={{0,2},{1,3},{2,0},{3,1},{4,6},{5,7},{6,4},{7,5},{8,10},{9,11},{10,... | collective-permute-start | bytes 7077896 | tf_op jit(solution)/shard_map/ppermute | solution.py:983
  250.7 264.2 %reduce-scatter.2.cloned.1.call-start = ((), (), s32[]{:S(2)}) async-start(), calls=%async_computation.3 | async-start | bytes 10948608 | tf_op jit(solution)/shard_map/reduce_scatter | solution.py:1185
  373.0 32.1 %collective-permute-start.14 = (bf16[8,48,2304]{2,1,0:T(8,128)(2,1)S(1)}, bf16[8,48,2304]{2,1,0:T(8,128)(2,1)}, u32[]{:S(2)}, u32[]{:S(2)}) collective-permute-start(bf16[8,48,2304]{2,1,0:T(8,128)(2,1)S(1)} %slice.250), channel_id=1, source_target_pairs={{0,2},{1,3},{2,0},{3,1},{4,6},{5,7},{6,4},{7,5},{8,10},{9,11},{10,... | collective-permute-start | bytes 5308424 | tf_op jit(solution)/shard_map/ppermute | solution.py:983
  415.7 40.7 %copy-start.2 = (bf16[64,1,768]{2,1,0:T(2,128)(2,1)S(1)}, bf16[64,1,768]{2,1,0:T(2,128)(2,1)}, u32[]{:S(2)}) copy-start(bf16[64,1,768]{2,1,0:T(2,128)(2,1)} %get-tuple-element.335) | copy-start | bytes 294916
  419.5 44.0 %collective-permute-start.15 = (bf16[4,48,2304]{2,1,0:T(8,128)(2,1)}, bf16[4,48,2304]{2,1,0:T(8,128)(2,1)}, u32[]{:S(2)}, u32[]{:S(2)}) collective-permute-start(bf16[4,48,2304]{2,1,0:T(8,128)(2,1)} %slice.256), channel_id=1, source_target_pairs={{0,8},{1,9},{2,6},{3,7},{4,12},{5,13},{6,2},{7,3},{8,0},{9,1},{10,... | collective-permute-start | bytes 2654216 | tf_op jit(solution)/shard_map/ppermute | solution.py:987
  448.1 13.3 %collective-permute-start.16 = (f32[16,16,24]{2,0,1:T(8,128)}, f32[16,16,24]{2,0,1:T(8,128)S(1)}, u32[]{:S(2)}, u32[]{:S(2)}) collective-permute-start(f32[16,16,24]{2,0,1:T(8,128)} %slice_select_fusion), channel_id=1, source_target_pairs={{0,16},{1,17},{2,18},{3,19},{4,20},{5,21},{6,22},{7,23},{8,24},{9,... | collective-permute-start | bytes 73736 | tf_op jit(solution)/shard_map/ppermute | solution.py:983
  448.2 18.6 %collective-permute-start.17 = (bf16[2,176,768]{2,1,0:T(8,128)(2,1)}, bf16[2,176,768]{2,1,0:T(8,128)(2,1)S(1)}, u32[]{:S(2)}, u32[]{:S(2)}) collective-permute-start(bf16[2,176,768]{2,1,0:T(8,128)(2,1)} %get-tuple-element.342), channel_id=1, source_target_pairs={{0,1},{1,0},{2,3},{3,2},{4,5},{5,4},{6,7},{7,6},{8,9},{9,8},{10,11... | collective-permute-start | bytes 1622024 | tf_op jit(solution)/shard_map/ppermute | solution.py:983
  452.7 35.0 %collective-permute-start.20 = (bf16[2,160,768]{2,1,0:T(8,128)(2,1)}, bf16[2,160,768]{2,1,0:T(8,128)(2,1)}, u32[]{:S(2)}, u32[]{:S(2)}) collective-permute-start(bf16[2,160,768]{2,1,0:T(8,128)(2,1)} %slice.272), channel_id=1, source_target_pairs={{0,1},{1,0},{2,3},{3,2},{4,5},{5,4},{6,7},{7,6},{8,9},{9,8},{10,11... | collective-permute-start | bytes 1474568 | tf_op jit(solution)/shard_map/ppermute | solution.py:983
  452.8 45.3 %collective-permute-start.23 = (bf16[2,176,768]{2,1,0:T(8,128)(2,1)}, bf16[2,176,768]{2,1,0:T(8,128)(2,1)}, u32[]{:S(2)}, u32[]{:S(2)}) collective-permute-start(bf16[2,176,768]{2,1,0:T(8,128)(2,1)} %get-tuple-element.341), channel_id=1, source_target_pairs={{0,1},{1,0},{2,3},{3,2},{4,5},{5,4},{6,7},{7,6},{8,9},{9,8},{10,11... | collective-permute-start | bytes 1622024 | tf_op jit(solution)/shard_map/ppermute | solution.py:983
  468.4 7.4 %collective-permute-start.19 = (f32[8,16,24]{2,0,1:T(8,128)S(1)}, f32[8,16,24]{2,0,1:T(8,128)S(1)}, u32[]{:S(2)}, u32[]{:S(2)}) collective-permute-start(f32[8,16,24]{2,0,1:T(8,128)S(1)} %slice_select_fusion.1), channel_id=1, source_target_pairs={{0,8},{1,9},{2,10},{3,11},{4,12},{5,13},{6,14},{7,15},{8,0},{9,1},... | collective-permute-start | bytes 36872 | tf_op jit(solution)/shard_map/ppermute | solution.py:983
  471.4 15.2 %collective-permute-start.18 = (bf16[2,48,2304]{2,1,0:T(8,128)(2,1)}, bf16[2,48,2304]{2,1,0:T(8,128)(2,1)}, u32[]{:S(2)}, u32[]{:S(2)}) collective-permute-start(bf16[2,48,2304]{2,1,0:T(8,128)(2,1)} %slice.269), channel_id=1, source_target_pairs={{0,16},{1,17},{2,10},{3,11},{4,20},{5,21},{6,14},{7,15},{8,24},{9,... | collective-permute-start | bytes 1327112 | tf_op jit(solution)/shard_map/ppermute | solution.py:987
  490.4 7.3 %collective-permute-start.22 = (f32[4,16,24]{2,0,1:T(4,128)S(1)}, f32[4,16,24]{2,0,1:T(4,128)S(1)}, u32[]{:S(2)}, u32[]{:S(2)}) collective-permute-start(f32[4,16,24]{2,0,1:T(4,128)S(1)} %slice_select_fusion.2), channel_id=1, source_target_pairs={{0,4},{1,5},{2,6},{3,7},{4,0},{5,1},{6,2},{7,3},{8,12},{9,13},{10,... | collective-permute-start | bytes 18440 | tf_op jit(solution)/shard_map/ppermute | solution.py:983
  492.1 6.0 %collective-permute-start.21 = (bf16[1,48,2304]{2,1,0:T(8,128)(2,1)S(1)}, bf16[1,48,2304]{2,1,0:T(8,128)(2,1)S(1)}, u32[]{:S(2)}, u32[]{:S(2)}) collective-permute-start(bf16[1,48,2304]{2,1,0:T(8,128)(2,1)S(1)} %slice.275), channel_id=1, source_target_pairs={{0,4},{1,5},{2,18},{3,19},{4,0},{5,1},{6,22},{7,23},{8,12},{9,13},... | collective-permute-start | bytes 663560 | tf_op jit(solution)/shard_map/ppermute | solution.py:987
  498.1 16.1 %collective-permute-start.26 = (bf16[1,24,2304]{2,1,0:T(8,128)(2,1)S(1)}, bf16[1,24,2304]{2,1,0:T(8,128)(2,1)S(1)}, u32[]{:S(2)}, u32[]{:S(2)}) collective-permute-start(bf16[1,24,2304]{2,1,0:T(8,128)(2,1)S(1)} %broadcast_select_fusion), channel_id=1, source_target_pairs={{0,1},{1,0},{2,3},{3,2},{4,5},{5,4},{6,7},{7,6},{8,9},{9,8},{10,11... | collective-permute-start | bytes 331784 | tf_op jit(solution)/shard_map/ppermute | solution.py:983
  499.8 1.3 collective-permute-start.24
  501.1 11.8 %collective-permute-start.25 = (f32[1,16,24]{2,0,1:T(1,128)S(1)}, f32[1,16,24]{2,0,1:T(1,128)S(1)}, u32[]{:S(2)}, u32[]{:S(2)}) collective-permute-start(f32[1,16,24]{2,0,1:T(1,128)S(1)} %broadcast_select_fusion.2), channel_id=1, source_target_pairs={{0,1},{1,0},{2,3},{3,2},{4,5},{5,4},{6,7},{7,6},{8,9},{9,8},{10,11... | collective-permute-start | bytes 4616 | tf_op jit(solution)/shard_map/ppermute | solution.py:983
  (9 other events, 92.8 us)
Sparse Core Ops, SparseCore 0:
  13.9 132.8 all-gather.2
  250.9 68.0 all-gather.4
  325.0 154.0 reduce-scatter.1
where the time goes:
time: 537 us; the launch traced here: 527 us
  Pallas kernels  253 us (47%)
  waiting for transfers between devices  83.8 us (16%)
  starting transfers between devices  74 us (14%)
  local copies, waits for them, and re-layouts  45.9 us (9%)
  other arithmetic  36.2 us (7%)
  between operations  30.3 us (6%)
    ppermute x9, waiting for transfers between devices, step(): return lax.ppermute(value, axes, pairs)  68.4 us
    ppermute x18, starting transfers between devices, swap(): return lax.ppermute(value, axes, [(i, i ^ bit) for i in range(self.count)])  39.7 us
    pallas_call x1, Pallas kernels, attend_back_call(): pl.pallas_call(functools.partial(attend_back_body, sz.images, sz.blocks),...  38.9 us
    pallas_call x1, Pallas kernels, back_call(): pl.pallas_call(back_body, grid_spec=pltpu.PrefetchScalarGridSpec(num_scal...  37.6 us
    pallas_call x1, Pallas kernels, mlp_call(): pl.pallas_call(mlp_body, grid_spec=pltpu.PrefetchScalarGridSpec(num_scala...  34.4 us
    ppermute x9, starting transfers between devices, step(): return lax.ppermute(value, axes, pairs)  34.2 us
    pallas_call x2, Pallas kernels, attend_call(): pl.pallas_call(functools.partial(attend_body, sz.images, sz.blocks, at),...  33.4 us
    pallas_call x1, Pallas kernels, outer_block_call(): pl.pallas_call(functools.partial(outer_block_body, sz.images, sz.blocks,...  28.6 us
  transfers between devices with their start and end apart: 30, of which 13 were waited for; matrix products, arithmetic and copies ran while one was open for 15% of the time, Pallas kernels for 43%

commit v1 on v0

--- a/solution.py
+++ b/solution.py
@@ -11,9 +11,13 @@
 HEAD_DIM = 64
 BLOCK = 256
 PAIR = 128
+SPAN = 512
+BACK_SPAN = 256
 wide = jnp.float32
 low = jnp.bfloat16
 masked_score = -1e30
+base_two = 1.4426950408889634
+score_scale = 0.125 * base_two
 norm_epsilon = 1e-06
 root_two_pi = 0.7978845608028654
 vmem_bytes = 60 * 1024 * 1024
@@ -274,36 +278,38 @@
 def attend_body(images, blocks, at, meta, q_ref, k_ref, v_ref, *rest):
     out_ref, lse_ref = rest[-2:]
     count, length = meta[at], meta[images + at]
-    lane = lax.broadcasted_iota(jnp.int32, (BLOCK, PAIR), 1)
-    first = lane < HEAD_DIM
 
     def variant(keys_in):
         near = keys_in - BLOCK
-        column = lax.broadcasted_iota(jnp.int32, (BLOCK, BLOCK), 1) + near
-
-        @pl.loop(0, count)
-        def _(step):
-            rows = pl.ds(pl.multiple_of(step * BLOCK, BLOCK), BLOCK)
+        start = 0
+        while start < keys_in:
+            size = min(SPAN, keys_in - start)
+            rows = slice(start, start + size)
+            start += size
+            lane = lax.broadcasted_iota(jnp.int32, (size, PAIR), 1)
+            first = lane < HEAD_DIM
+            column = lax.broadcasted_iota(jnp.int32, (size, BLOCK), 1) + near
             q = q_ref[rows, :]
             outs, logs = [], []
             for head in range(2):
                 own = first if head == 0 else jnp.logical_not(first)
                 qh = jnp.where(own, q, jnp.zeros_like(q))
-                last = dot_nt(qh, k_ref[near:keys_in, :]) * 0.125
+                last = dot_nt(qh, k_ref[near:keys_in, :])
                 last = jnp.where(column < length, last, masked_score)
                 top = jnp.max(last, axis=1, keepdims=True)
                 if near:
-                    body = dot_nt(qh, k_ref[:near, :]) * 0.125
+                    body = dot_nt(qh, k_ref[:near, :])
                     top = jnp.maximum(top, jnp.max(body, axis=1, keepdims=True))
-                p_last = jnp.exp(last - top)
-                total = jnp.sum(p_last, axis=1, keepdims=True)
-                acc = dot_nn(p_last.astype(low), v_ref[near:keys_in, :])
+                drop = top * score_scale
+                share = jnp.exp2(last * score_scale - drop)
+                total = jnp.sum(share, axis=1, keepdims=True)
+                acc = dot_nn(share.astype(low), v_ref[near:keys_in, :])
                 if near:
-                    p_body = jnp.exp(body - top)
-                    total = total + jnp.sum(p_body, axis=1, keepdims=True)
-                    acc = acc + dot_nn(p_body.astype(low), v_ref[:near, :])
+                    share = jnp.exp2(body * score_scale - drop)
+                    total = total + jnp.sum(share, axis=1, keepdims=True)
+                    acc = acc + dot_nn(share.astype(low), v_ref[:near, :])
                 outs.append(acc / total)
-                logs.append(top + jnp.log(total))
+                logs.append(drop + jnp.log2(total))
             out_ref[rows, :] = jnp.where(first, outs[0], outs[1]).astype(low)
             both = jnp.where(lane == 0, logs[0], logs[1])
             lse_ref[0, :, rows] = both.T[:8, :]
@@ -581,6 +587,84 @@
         cost_estimate=cost(16 * 8 * w * f, sz.rows * w * 2 + 4 * w * f + 8 * w * w),
         name="head",
     )(meta, *ins, block, *weight)
+
+
+def owner_body(own, fold, at, rows, probe, g_fc2, g_fc1, g_out, g_kv, sums, wide_rows, near, far):
+    count, _, width = rows.shape
+    group = HEAD_ROWS
+    select = lax.broadcasted_iota(jnp.int32, (width, PAIR), 1)
+    source = lax.broadcasted_iota(jnp.int32, (width, PAIR), 0)
+    select = jnp.where((source == at[0] * own + select) & (select < own), 1.0, 0.0).astype(low)
+
+    def rows_of(k):
+        return rows[:, k * group : (k + 1) * group, :]
+
+    def every(ref, r):
+        return ref[pl.ds(r, count, stride=group), :].astype(low)
+
+    def full(r):
+        at_row = pl.ds(r - 2 * group, count, stride=group)
+        return jnp.concatenate(
+            [wide_rows[c, at_row, :] for c in range(width // PAIR)], axis=1
+        ).astype(low)
+
+    near[...] = dot_nn(rows_of(0).reshape(count * group, width), select)
+    last = rows_of(2).reshape(count * group, width)
+    far[...] = dot_nn(last, select)
+    for c in range(width // PAIR):
+        wide_rows[c] = last[:, c * PAIR : (c + 1) * PAIR].astype(wide)
+    mixed = jnp.sum(rows_of(1).astype(wide), axis=0)
+    sums[:group, :] = mixed
+    sums[group:, :] = jnp.sum(rows_of(2).astype(wide), axis=0)
+    cot = full(SENT_COT)
+    normed = every(far, SENT_NORMED - 2 * group)
+    for j in range(fold):
+        g_fc2[j] = dot_tn(every(far, SENT_ACT + j - 2 * group), cot)[:own]
+        g_fc1[:, j * width : (j + 1) * width] = dot_tn(normed, full(SENT_GRAD + j))[:own]
+    g_out[...] = dot_tn(every(far, SENT_POOLED - 2 * group), full(SENT_BRANCH))[:own]
+    pull = full(SENT_PULL)
+    first = lax.broadcasted_iota(jnp.int32, (PAIR, PAIR), 1) < HEAD_DIM
+    for p in range(width // PAIR):
+        piece = pull[:, p * PAIR : (p + 1) * PAIR]
+        both = [dot_tn(every(near, 2 * p + k), piece) for k in range(2)]
+        at_cols = slice(width + p * PAIR, width + (p + 1) * PAIR)
+        g_kv[:, at_cols] = jnp.where(first, both[0], both[1])[:own]
+    head_row = lax.broadcasted_iota(jnp.int32, (group, width), 0)
+    head_col = lax.broadcasted_iota(jnp.int32, (group, width), 1) // HEAD_DIM
+    query = jnp.broadcast_to(probe[HEADS : HEADS + 1, :], (group, width))
+    query = jnp.where(head_row == head_col, query, 0.0).astype(low)
+    top, rest = halves(mixed)
+    top, rest = halves(dot_nn(top, select) + dot_nn(rest, select))
+    g_kv[:, :width] = 0.125 * (dot_tn(top, query) + dot_tn(rest, query))[:own]
+
+
+def owner_call(at, rows, probe_w, own, fold):
+    count, _, width = rows.shape
+    shapes = [
+        jax.ShapeDtypeStruct(shape, wide)
+        for shape in (
+            (fold, own, width), (own, fold * width), (own, width), (own, 2 * width),
+            (2 * HEAD_ROWS, width),
+        )
+    ]
+    return pl.pallas_call(
+        functools.partial(owner_body, own, fold),
+        grid_spec=pltpu.PrefetchScalarGridSpec(
+            num_scalar_prefetch=1,
+            grid=(1,),
+            in_specs=[whole(rows.shape), whole(probe_w.shape)],
+            out_specs=[pl.BlockSpec(s.shape, lambda *_, r=len(s.shape): (0,) * r) for s in shapes],
+            scratch_shapes=[
+                pltpu.VMEM((width // PAIR, count * HEAD_ROWS, PAIR), wide),
+                pltpu.VMEM((count * HEAD_ROWS, PAIR), wide),
+                pltpu.VMEM((count * HEAD_ROWS, PAIR), wide),
+            ],
+        ),
+        out_shape=shapes,
+        compiler_params=params(1),
+        cost_estimate=cost(64 * count * width * PAIR, 8 * rows.size),
+        name="owner",
+    )(at, rows, probe_w)
 
 
 def back_body(
@@ -827,24 +911,21 @@
 
     def variant(keys_in):
         near = keys_in - BLOCK
-        valid = lax.broadcasted_iota(jnp.int32, (BLOCK, BLOCK), 0) + near < length
         keys = k_ref[:keys_in, :]
         kept_keys = [keep(keys, head) for head in range(2)]
         values = v_ref[:keys_in, :]
         kept_values = [keep(values, head) for head in range(2)]
-        dk_acc[:keys_in, :] = jnp.zeros((keys_in, PAIR), wide)
-        dv_acc[:keys_in, :] = jnp.zeros((keys_in, PAIR), wide)
-
-        @pl.loop(0, count)
-        def _(step):
-            rows = pl.ds(pl.multiple_of(step * BLOCK, BLOCK), BLOCK)
+        start = 0
+        while start < keys_in:
+            size = min(BACK_SPAN, keys_in - start)
+            rows = slice(start, start + size)
+            valid = lax.broadcasted_iota(jnp.int32, (BLOCK, size), 0) + near < length
             q, g = q_ref[rows, :], g_ref[rows, :]
-            dq = None
+            dq = dk = dv = None
             for head in range(2):
                 log = lse_ref[0, head : head + 1, rows]
                 drop = delta_ref[0, head : head + 1, rows]
-                score = dot_nt(kept_keys[head], q) * 0.125
-                share = jnp.exp(score - log)
+                share = jnp.exp2(dot_nt(kept_keys[head], q) * score_scale - log)
                 if near:
                     share = jnp.concatenate(
                         [share[:near], jnp.where(valid, share[near:], 0.0)], axis=0
@@ -853,14 +934,25 @@
                     share = jnp.where(valid, share, 0.0)
                 reach = dot_nt(kept_values[head], g)
                 grad = (share * (reach - drop)).astype(low)
-                dv_acc[:keys_in, :] += dot_nn(share.astype(low), keep(g, head))
-                dk_acc[:keys_in, :] += dot_nn(grad, keep(q, head))
-                term = dot_tn(grad, kept_keys[head])
-                dq = term if dq is None else dq + term
+                terms = (
+                    dot_tn(grad, kept_keys[head]),
+                    dot_nn(grad, keep(q, head)),
+                    dot_nn(share.astype(low), keep(g, head)),
+                )
+                if head == 0:
+                    dq, dk, dv = terms
+                else:
+                    dq, dk, dv = dq + terms[0], dk + terms[1], dv + terms[2]
             dq_ref[rows, :] = (dq * 0.125).astype(low)
-
-        dk_ref[:keys_in, :] = (dk_acc[:keys_in, :] * 0.125).astype(low)
-        dv_ref[:keys_in, :] = dv_acc[:keys_in, :].astype(low)
+            if start > 0:
+                dk, dv = dk + dk_acc[:keys_in, :], dv + dv_acc[:keys_in, :]
+            start += size
+            if start < keys_in:
+                dk_acc[:keys_in, :] = dk
+                dv_acc[:keys_in, :] = dv
+            else:
+                dk_ref[:keys_in, :] = (dk * 0.125).astype(low)
+                dv_ref[:keys_in, :] = dv.astype(low)
 
     for keys in range(1, blocks + 1):
         pl.when(count == keys)(functools.partial(variant, keys * BLOCK))
@@ -1207,39 +1299,15 @@
         given = lax.all_to_all(patch_low, "seq", split_axis=1, concat_axis=0, tiled=True)[::share]
 
     def head_part(rows):
-        narrow = own_part(rows.reshape(count * images, SENT_ROWS, width))
         rows = rows.reshape(count * images, SENT_ROWS, width)
-        act_own = narrow[:, SENT_ACT : SENT_ACT + fold].transpose(0, 2, 1).reshape(-1, per)
-        grad_pool_v = jnp.einsum(
-            "ihr,ihd->rhd",
-            narrow[:, :HEADS],
-            rows[:, SENT_PULL].reshape(-1, HEADS, HEAD_DIM),
-            preferred_element_type=wide,
-        ).reshape(own, width)
-        return (
-            dot_tn(act_own, rows[:, SENT_COT]),
-            dot_tn(narrow[:, SENT_POOLED], rows[:, SENT_BRANCH]),
-            grad_pool_v,
-            narrow[:, SENT_NORMED],
-            jnp.sum(narrow[:, SENT_MIX : SENT_MIX + HEADS].astype(wide), axis=0),
-        )
-
-    def hidden_part(rows, normed_own):
-        rows = rows.reshape(count * images, SENT_ROWS, width)
-        head_grad = rows[:, SENT_GRAD : SENT_GRAD + fold].reshape(count * images, hidden)
-        return by_column(dot_tn(normed_own, head_grad))
-
-    def sums_part(rows, mix_own):
-        rows = rows.reshape(count * images, SENT_ROWS, width)
-        row_sums = jnp.sum(rows[:, 2 * HEAD_ROWS - 1 :].astype(wide), axis=0)
-        query_grad = row_sums[SENT_QUERY - 2 * HEAD_ROWS + 1] + row_sums[0]
-        pool_query = probe_w[HEADS]
-        grad_pool_k = (
-            0.125 * mix_own.T[:, :, None] * pool_query.reshape(1, HEADS, HEAD_DIM)
-        ).reshape(own, width)
-        pooled = rows[:, SENT_OUT].astype(wide) + rows[:, SENT_OUT_REST].astype(wide)
-        pooled = pooled.reshape(img_count, seq_count, images, width)[:, ::share]
-        pooled = lax.dynamic_index_in_dim(pooled, me // seq_count, 0, keepdims=False)
+        return owner_call(me[None].astype(jnp.int32), rows, probe_w, own, fold)
+
+    def sums_part(rows, row_sums):
+        rows = lax.dynamic_slice_in_dim(
+            rows.reshape(img_count, seq_count, images, SENT_ROWS, width), me // seq_count, 1
+        )[0, ::share]
+        query_grad = row_sums[SENT_QUERY - HEAD_ROWS] + row_sums[SENT_QUERY_REST - HEAD_ROWS]
+        pooled = rows[:, :, SENT_OUT].astype(wide) + rows[:, :, SENT_OUT_REST].astype(wide)
         pooled = pooled.reshape(groups, width)
         pooled = jnp.concatenate(
             [lax.dynamic_slice_in_dim(pooled, slot_of[k], 1) for k in range(groups)], axis=0
@@ -1248,7 +1316,6 @@
             pooled,
             probe_vector.astype(wide)[:, None] * query_grad[None, :],
             jnp.sum(pool_query_weight.astype(wide) * query_grad[None, :], axis=1),
-            grad_pool_k,
             own_part(query_grad),
             own_part(row_sums),
         )
@@ -1263,18 +1330,17 @@
         if tick == 0:
             made.append(head_part(rows))
         elif tick == 1:
-            made.append(hidden_part(rows, made[0][3]))
-        elif tick == 2:
             made.append(sums_part(rows, made[0][4]))
         last, sums, rows, taken, made = together(last, sums, rows, taken, made)
-    (grad_head_fc2, grad_pool_out, grad_pool_v, _, _), grad_head_fc1, made = made
-    pooled, grad_pool_query_weight, grad_probe, grad_pool_k, g_pool_query_bias, own_sums = made
-    grad_pool_kv = jnp.concatenate([grad_pool_k, grad_pool_v], axis=1)
+    (grad_head_fc2, grad_head_fc1, grad_pool_out, grad_pool_kv, _), made = made
+    grad_head_fc2 = grad_head_fc2.transpose(1, 0, 2).reshape(per, width)
+    grad_head_fc1 = by_column(grad_head_fc1)
+    pooled, grad_pool_query_weight, grad_probe, g_pool_query_bias, own_sums = made
 
     def own_sum(at):
-        return own_sums[at - 2 * HEAD_ROWS + 1]
-
-    g_head_fc1_bias = own_sums[SENT_GRAD - 2 * HEAD_ROWS + 1 :][:fold].T.reshape(per)
+        return own_sums[at - HEAD_ROWS]
+
+    g_head_fc1_bias = own_sums[SENT_GRAD - HEAD_ROWS :][:fold].T.reshape(per)
     last = last.reshape(seq_count, own, 3 * width)
     for bit in reversed(wires.seq_bits):
         last = wires.small_half(last, me, bit)

time: 537 us -> 550 us (1.024)
  Pallas kernels: 253 us -> 279 us
  waiting for transfers between devices: 83.8 us -> 100 us
  local copies, waits for them, and re-layouts: 45.9 us -> 32.1 us
  other arithmetic: 36.2 us -> 29.2 us
  starting transfers between devices: 74 us -> 68.4 us
    ppermute x9, starting transfers between devices: 34.2 us -> 7.85 us  [step(): return lax.ppermute(value, axes, pairs)]
    ppermute x18, starting transfers between devices: 39.7 us -> 60.4 us  [swap(): return lax.ppermute(value, axes, [(i, i ^ bit) for i in range(self.count)])]
    pallas_call x1, Pallas kernels: 38.9 us -> 52 us  [attend_back_call(): pl.pallas_call(functools.partial(attend_back_body, sz.images, sz.blocks),...]
    ppermute x18, waiting for transfers between devices: 14.1 us -> 26.5 us  [swap(): return lax.ppermute(value, axes, [(i, i ^ bit) for i in range(self.count)])]
    slice x6 -> x0, local copies, waits for them, and re-layouts: 10.9 us -> none  [the longest x1 3.34 us: head_part(): rows[:, SENT_PULL].reshape(-1, HEADS, HEAD_DIM)]
    pallas_call x0 -> x1, Pallas kernels: none -> 5.75 us  [owner_call(): pl.pallas_call(functools.partial(owner_body, own, fold), grid_spec=pltpu....]
  transfers between devices with their start and end apart: 30 -> 30, of which waited for: 13 -> 13; matrix products, arithmetic and copies ran while one was open for 15% -> 10% of each run, Pallas kernels for 43% -> 46%
where the time goes in v1:
time: 550 us; the launch traced here: 539 us
  Pallas kernels  279 us (51%)
  waiting for transfers between devices  100 us (18%)
  starting transfers between devices  68.4 us (12%)
  local copies, waits for them, and re-layouts  32.1 us (6%)
  between operations  30.2 us (5%)
  other arithmetic  29.2 us (5%)
    ppermute x9, waiting for transfers between devices, step(): return lax.ppermute(value, axes, pairs)  73.8 us
    ppermute x18, starting transfers between devices, swap(): return lax.ppermute(value, axes, [(i, i ^ bit) for i in range(self.count)])  60.4 us
    pallas_call x1, Pallas kernels, attend_back_call(): pl.pallas_call(functools.partial(attend_back_body, sz.images, sz.blocks),...  52 us
    pallas_call x1, Pallas kernels, back_call(): pl.pallas_call(back_body, grid_spec=pltpu.PrefetchScalarGridSpec(num_scal...  39 us
    pallas_call x1, Pallas kernels, mlp_call(): pl.pallas_call(mlp_body, grid_spec=pltpu.PrefetchScalarGridSpec(num_scala...  37.6 us
    pallas_call x2, Pallas kernels, attend_call(): pl.pallas_call(functools.partial(attend_body, sz.images, sz.blocks, at),...  32.8 us
    pallas_call x1, Pallas kernels, outer_block_call(): pl.pallas_call(functools.partial(outer_block_body, sz.images, sz.blocks,...  30.2 us
    ppermute x18, waiting for transfers between devices, swap(): return lax.ppermute(value, axes, [(i, i ^ bit) for i in range(self.count)])  26.5 us
  transfers between devices with their start and end apart: 30, of which 13 were waited for; matrix products, arithmetic and copies ran while one was open for 10% of the time, Pallas kernels for 46%

profile of v1, /device:TPU:0, one launch (start us, length us, event | category | flops | bytes accessed | tf_op | source)
XLA Modules:
  0.0 539.4 jit_solution(7531803675746281752)
XLA Ops:
  10.1 3.6 packs.1
  13.8 3.0 collective-permute-start
  32.2 3.8 collective-permute-done.1
  36.9 5.1 collective-permute-done.2
  47.5 16.7 %collective-permute-done.3 = bf16[2,48,2432]{2,1,0:T(8,128)(2,1)} collective-permute-done((bf16[2,48,2432]{2,1,0:T(8,128)(2,1)}, bf16[2,48,2432]{2,1,0:T(8,128)(2,1)}, u32[]{:S(2)}, u32[]{:S(2)}) %collective-permute-start.3) | collective-permute-done | bytes 466976 | tf_op jit(solution)/shard_map/ppermute | solution.py:1079
  65.5 3.1 collective-permute-start.5
  70.4 17.4 %collective-permute-done.5 = bf16[4,48,2432]{2,1,0:T(8,128)(2,1)S(1)} collective-permute-done((bf16[4,48,2432]{2,1,0:T(8,128)(2,1)S(1)}, bf16[4,48,2432]{2,1,0:T(8,128)(2,1)S(1)}, u32[]{:S(2)}, u32[]{:S(2)}) %collective-permute-start.5) | collective-permute-done | bytes 933920 | tf_op jit(solution)/shard_map/ppermute | solution.py:1079
  90.9 4.1 maximum_select_fusion
  95.0 6.5 %collective-permute-start.8 = (bf16[24,6144]{1,0:T(8,128)(2,1)S(1)}, bf16[24,6144]{1,0:T(8,128)(2,1)S(1)}, u32[]{:S(2)}, u32[]{:S(2)}) collective-permute-start(bf16[24,6144]{1,0:T(8,128)(2,1)S(1)} %copy-done.3), channel_id=1, source_target_pairs={{0,1},{1,0},{2,3},{3,2},{4,5},{5,4},{6,7},{7,6},{8,9},{9,8},{10,11... | collective-permute-start | bytes 884744 | tf_op jit(solution)/shard_map/ppermute | solution.py:1075
  101.6 13.7 %qkv.1 = (bf16[2048,2304]{1,0:T(8,128)(2,1)}, bf16[2048,768]{1,0:T(8,128)(2,1)}, f32[32,768]{1,0:T(8,128)}) custom-call(s32[36]{0:T(128)} %concatenate.111.meta, bf16[2048,768]{1,0:T(8,128)(2,1)} %bitcast.142, bf16[8,48,2432]{2,1,0:T(8,128)(2,1)} %pad_maximum_fusion.2.mine, bf16[8,48,2432]{2,1,0:T(8,128)(2,1)} %collective-permute-done.7.theirs), custom_call_target="tpu_custom_call" | custom-call | flops 7247757312 | bytes 19267584 | tf_op jit(solution)/shard_map/qkv/pallas_call | solution.py:254
  115.6 2.6 collective-permute-start.9
  118.2 22.6 %attend_0.1 = (bf16[2048,768]{1,0:T(8,128)(2,1)}, f32[2,48,1024]{2,1,0:T(8,128)}) custom-call(s32[36]{0:T(128)} %concatenate.111.meta, bf16[2048,2304]{1,0:T(8,128)(2,1)} %get-tuple-element.157.q_ref.k_ref.v_ref, bf16[2048,2304]{1,0:T(8,128)(2,1)} %get-tuple-element.157.q_ref.k_ref.v_ref, bf16[2048,2304]{1,0:T(8,128)(2,1)} %get-tuple-element.157.q_ref.k_ref.v_ref), custom_call_target="tpu_custom_call" | custom-call | flops 3221225472 | bytes 6291456 | tf_op jit(solution)/shard_map/attend_0/pallas_call | solution.py:327
  141.0 10.2 %attend_1.1 = (bf16[2048,768]{1,0:T(8,128)(2,1)}, f32[2,48,1024]{2,1,0:T(8,128)}) custom-call(s32[36]{0:T(128)} %concatenate.111.meta, bf16[2048,2304]{1,0:T(8,128)(2,1)} %get-tuple-element.157.q_ref.k_ref.v_ref, bf16[2048,2304]{1,0:T(8,128)(2,1)} %get-tuple-element.157.q_ref.k_ref.v_ref, ...), custom_call_target="tpu_custom_call", output_to_operand_aliasing={{0}: (4, {}), {1}: (5, {})} | custom-call | flops 3221225472 | bytes 6291456 | tf_op jit(solution)/shard_map/attend_1/pallas_call | solution.py:327
  151.2 18.7 %collective-permute-done.10 = bf16[2,48,6144]{2,1,0:T(8,128)(2,1)} collective-permute-done((bf16[2,48,6144]{2,1,0:T(8,128)(2,1)S(1)}, bf16[2,48,6144]{2,1,0:T(8,128)(2,1)}, u32[]{:S(2)}, u32[]{:S(2)}) %collective-permute-start.10) | collective-permute-done | bytes 1179680 | tf_op jit(solution)/shard_map/ppermute | solution.py:1079
  171.4 12.4 %collective-permute-start.11 = (bf16[4,48,6144]{2,1,0:T(8,128)(2,1)S(1)}, bf16[4,48,6144]{2,1,0:T(8,128)(2,1)}, u32[]{:S(2)}, u32[]{:S(2)}) collective-permute-start(bf16[4,48,6144]{2,1,0:T(8,128)(2,1)S(1)} %pad_maximum_fusion.1), channel_id=1, source_target_pairs={{0,2},{1,3},{2,0},{3,1},{4,6},{5,7},{6,4},{7,5},{8,10},{9,11},{10,... | collective-permute-start | bytes 7077896 | tf_op jit(solution)/shard_map/ppermute | solution.py:1075
  183.9 37.6 %mlp.1 = (f32[2048,768]{1,0:T(8,128)}, bf16[2048,768]{1,0:T(8,128)(2,1)}, bf16[2048,3072]{1,0:T(8,128)(2,1)}, bf16[2048,3072]{1,0:T(8,128)(2,1)}, f32[2048,768]{1,0:T(8,128)}, /*index=5*/bf16[2048,768]{1,0:T(8,128)(2,1)}) custom-call(s32[36]{0:T(128)} %concatenate.111.meta, bf16[2048,768]{1,0:T(8,128)(2,1)} %bitcast.143, ...), custom_call_target="tpu_custom_call" | custom-call | flops 21743271936 | bytes 56623104 | tf_op jit(solution)/shard_map/mlp/pallas_call | solution.py:392
  222.3 4.2 pad_maximum_fusion.mine
  226.5 25.7 %head.1 = (f32[2,16,1024]{2,1,0:T(8,128)}, f32[2,16,1024]{2,1,0:T(8,128)}, f32[2,16,768]{2,1,0:T(8,128)}, f32[16,768]{1,0:T(8,128)}, bf16[96,768]{1,0:T(8,128)(2,1)}, /*index=5*/f32[8,768]{1,0:T(8,128)}) custom-call(s32[36]{0:T(128)} %concatenate.111.meta, bf16[2048,768]{1,0:T(8,128)(2,1)} %get-tuple-element.171.fin, f32[16,768]{1,0:T(8,128)} %select_maximum_fusion.cot_ref, ...), custom_call_target="tpu_custom_call" | custom-call | flops 301989888 | bytes 17301504 | tf_op jit(solution)/shard_map/head/pallas_call | solution.py:569
  253.1 39.0 %mlp_back.1 = (bf16[2048,768]{1,0:T(8,128)(2,1)}, bf16[2048,3072]{1,0:T(8,128)(2,1)}, f32[2048,768]{1,0:T(8,128)}, bf16[2048,768]{1,0:T(8,128)(2,1)}, bf16[2048,...) custom-call(s32[36]{0:T(128)} %concatenate.111.meta, bf16[2048,768]{1,0:T(8,128)(2,1)} %get-tuple-element.171.fin, ...), custom_call_target="tpu_custom_call" | custom-call | flops 21743271936 | bytes 69206016 | tf_op jit(solution)/shard_map/mlp_back/pallas_call | solution.py:740
  292.1 30.2 %grad_block.1 = bf16[768,6912]{1,0:T(8,128)(2,1)} custom-call(s32[36]{0:T(128)} %concatenate.111.meta, bf16[2048,768]{1,0:T(8,128)(2,1)} %get-tuple-element.166.att.att_ref, bf16[2048,768]{1,0:T(8,128)(2,1)} %get-tuple-element.183.g_att_ref, bf16[2048,768]{1,0:T(8,128)(2,1)} %get-tuple-element.184.n2_ref, ...), custom_call_target="tpu_custom_call" | custom-call | flops 21743271936 | bytes 37748736 | tf_op jit(solution)/shard_map/grad_block/pallas_call | solution.py:818
  322.4 52.0 %attend_back.1 = (bf16[2048,768]{1,0:T(8,128)(2,1)}, bf16[2048,768]{1,0:T(8,128)(2,1)}, bf16[2048,768]{1,0:T(8,128)(2,1)}) custom-call(s32[36]{0:T(128)} %concatenate.111.meta, bf16[2048,2304]{1,0:T(8,128)(2,1)} %get-tuple-element.157.q_ref.k_ref.v_ref, bf16[2048,2304]{1,0:T(8,128)(2,1)} %get-tuple-element.157.q_ref.k_ref.v_ref, ...), custom_call_target="tpu_custom_call" | custom-call | flops 16106127360 | bytes 22020096 | tf_op jit(solution)/shard_map/attend_back/pallas_call | solution.py:969
  374.4 14.2 %grad_qkv.1 = bf16[16,48,2304]{2,1,0:T(8,128)(2,1)} custom-call(s32[36]{0:T(128)} %concatenate.111.meta, bf16[2048,768]{1,0:T(8,128)(2,1)} %get-tuple-element.182.n1_ref, bf16[2048,768]{1,0:T(8,128)(2,1)} %get-tuple-element.193.dq_ref.dq, bf16[2048,768]{1,0:T(8,128)(2,1)} %get-tuple-element.194.dk_ref.dk, bf16[2048,768]{1,0:T(8,128)(2,1)} %get-tuple-element.195.dv_ref.dv), custom_call_target="tpu_custom_call" | custom-call | flops 7247757312 | bytes 12582912 | tf_op jit(solution)/shard_map/grad_qkv/pallas_call | solution.py:843
  391.2 17.5 %qkv_back.1 = (f32[2048,768]{1,0:T(8,128)}, bf16[2048,768]{1,0:T(8,128)(2,1)}, f32[8,768]{1,0:T(8,128)}) custom-call(s32[36]{0:T(128)} %concatenate.111.meta, bf16[2048,768]{1,0:T(8,128)(2,1)} %bitcast.144, f32[2048,768]{1,0:T(8,128)} %get-tuple-element.199.g_res, bf16[2048,768]{1,0:T(8,128)(2,1)} %get-tuple-element.193.dq_ref.dq, ...), custom_call_target="tpu_custom_call" | custom-call | flops 7247757312 | bytes 31850496 | tf_op jit(solution)/shard_map/qkv_back/pallas_call | solution.py:1024
  424.7 4.0 collective-permute-start.16
  430.6 3.2 collective-permute-start.17
  433.9 5.8 %owner.1 = (f32[4,24,768]{2,1,0:T(8,128)}, f32[24,3072]{1,0:T(8,128)}, f32[24,768]{1,0:T(8,128)}, f32[24,1536]{1,0:T(8,128)}, f32[32,768]{1,0:T(8,128)}) custom-call(s32[1]{0:T(128)} %bitcast.62.at, bf16[64,48,768]{2,1,0:T(8,128)(2,1)} %bitcast.140, f32[16,768]{1,0:T(8,128)} %get-tuple-element.180.probe_w.probe), custom_call_target="tpu_custom_call" | custom-call | flops 402653184 | bytes 18874368 | tf_op jit(solution)/shard_map/owner/pallas_call | solution.py:650
  440.9 13.9 %collective-permute-done.17 = bf16[2,176,768]{2,1,0:T(8,128)(2,1)S(1)} collective-permute-done((bf16[2,176,768]{2,1,0:T(8,128)(2,1)}, bf16[2,176,768]{2,1,0:T(8,128)(2,1)S(1)}, u32[]{:S(2)}, u32[]{:S(2)}) %collective-permute-start.17) | collective-permute-done | bytes 540704 | tf_op jit(solution)/shard_map/ppermute | solution.py:1075
  462.3 12.5 %collective-permute-done.18 = bf16[2,48,2304]{2,1,0:T(8,128)(2,1)S(1)} collective-permute-done((bf16[2,48,2304]{2,1,0:T(8,128)(2,1)S(1)}, bf16[2,48,2304]{2,1,0:T(8,128)(2,1)S(1)}, u32[]{:S(2)}, u32[]{:S(2)}) %collective-permute-start.18) | collective-permute-done | bytes 442400 | tf_op jit(solution)/shard_map/ppermute | solution.py:1079
  474.9 24.7 %collective-permute-start.22 = (f32[4,16,24]{2,0,1:T(4,128)S(1)}, f32[4,16,24]{2,0,1:T(4,128)S(1)}, u32[]{:S(2)}, u32[]{:S(2)}) collective-permute-start(f32[4,16,24]{2,0,1:T(4,128)S(1)} %slice_select_fusion.2), channel_id=1, source_target_pairs={{0,4},{1,5},{2,6},{3,7},{4,0},{5,1},{6,2},{7,3},{8,12},{9,13},{10,... | collective-permute-start | bytes 18440 | tf_op jit(solution)/shard_map/ppermute | solution.py:1075
  501.5 4.7 collective-permute-done.21
  506.3 3.5 collective-permute-done.23
  518.5 6.9 %place.1 = f32[4,512,768]{2,1,0:T(8,128)} custom-call(s32[9]{0:T(128)} %pad_add_fusion.1.at, f32[2,2,512,768]{3,2,1,0:T(8,128)} %bitcast.137, bf16[2,512,768]{2,1,0:T(8,128)(2,1)} %pad_maximum_fusion.4.taken), custom_call_target="tpu_custom_call" | custom-call | bytes 15728640 | tf_op jit(solution)/shard_map/place/pallas_call | solution.py:877
  (165 shorter events, 65.9 us)
Async XLA Ops:
  7.2 176.7 %all-gather.3.cloned.1.call-start = ((), (), s32[]{:S(2)}) async-start(), calls=%async_computation.1 | async-start | bytes 15814656 | tf_op jit(solution)/shard_map/all_gather | solution.py:1210
  13.8 308.6 %all-gather.5.cloned.1.call-start = ((), (), s32[]{:S(2)}) async-start(), calls=%async_computation.2 | async-start | bytes 4866048 | tf_op jit(solution)/shard_map/all_gather | solution.py:1270
  13.8 15.3 %collective-permute-start = (bf16[24,2432]{1,0:T(8,128)(2,1)}, bf16[24,2432]{1,0:T(8,128)(2,1)S(1)}, u32[]{:S(2)}, u32[]{:S(2)}) collective-permute-start(bf16[24,2432]{1,0:T(8,128)(2,1)} %get-tuple-element.140), channel_id=1, source_target_pairs={{0,1},{1,0},{2,3},{3,2},{4,5},{5,4},{6,7},{7,6},{8,9},{9,8},{10,11... | collective-permute-start | bytes 350216 | tf_op jit(solution)/shard_map/ppermute | solution.py:1075
  29.9 6.1 %collective-permute-start.1 = (bf16[1,48,2432]{2,1,0:T(8,128)(2,1)S(1)}, bf16[1,48,2432]{2,1,0:T(8,128)(2,1)S(1)}, u32[]{:S(2)}, u32[]{:S(2)}) collective-permute-start(bf16[1,48,2432]{2,1,0:T(8,128)(2,1)S(1)} %maximum_select_fusion.2), channel_id=1, source_target_pairs={{0,4},{1,5},{2,18},{3,19},{4,0},{5,1},{6,22},{7,23},{8,12},{9,13},... | collective-permute-start | bytes 700424 | tf_op jit(solution)/shard_map/ppermute | solution.py:1079
  31.4 10.5 %collective-permute-start.2 = (bf16[2,112,768]{2,1,0:T(8,128)(2,1)S(1)}, bf16[2,112,768]{2,1,0:T(8,128)(2,1)S(1)}, u32[]{:S(2)}, u32[]{:S(2)}) collective-permute-start(bf16[2,112,768]{2,1,0:T(8,128)(2,1)S(1)} %slice.211), channel_id=1, source_target_pairs={{0,1},{1,0},{2,3},{3,2},{4,5},{5,4},{6,7},{7,6},{8,9},{9,8},{10,11... | collective-permute-start | bytes 1032200 | tf_op jit(solution)/shard_map/ppermute | solution.py:1075
  41.9 22.3 %collective-permute-start.3 = (bf16[2,48,2432]{2,1,0:T(8,128)(2,1)}, bf16[2,48,2432]{2,1,0:T(8,128)(2,1)}, u32[]{:S(2)}, u32[]{:S(2)}) collective-permute-start(bf16[2,48,2432]{2,1,0:T(8,128)(2,1)} %pad_maximum_fusion.7), channel_id=1, source_target_pairs={{0,16},{1,17},{2,10},{3,11},{4,20},{5,21},{6,14},{7,15},{8,24},{9,... | collective-permute-start | bytes 1400840 | tf_op jit(solution)/shard_map/ppermute | solution.py:1079
  43.1 22.5 %collective-permute-start.4 = (bf16[2,176,768]{2,1,0:T(8,128)(2,1)}, bf16[2,176,768]{2,1,0:T(8,128)(2,1)}, u32[]{:S(2)}, u32[]{:S(2)}) collective-permute-start(bf16[2,176,768]{2,1,0:T(8,128)(2,1)} %slice.212), channel_id=1, source_target_pairs={{0,1},{1,0},{2,3},{3,2},{4,5},{5,4},{6,7},{7,6},{8,9},{9,8},{10,11... | collective-permute-start | bytes 1622024 | tf_op jit(solution)/shard_map/ppermute | solution.py:1075
  65.5 22.2 %collective-permute-start.5 = (bf16[4,48,2432]{2,1,0:T(8,128)(2,1)S(1)}, bf16[4,48,2432]{2,1,0:T(8,128)(2,1)S(1)}, u32[]{:S(2)}, u32[]{:S(2)}) collective-permute-start(bf16[4,48,2432]{2,1,0:T(8,128)(2,1)S(1)} %pad_maximum_fusion.6), channel_id=1, source_target_pairs={{0,8},{1,9},{2,6},{3,7},{4,12},{5,13},{6,2},{7,3},{8,0},{9,1},{10,... | collective-permute-start | bytes 2801672 | tf_op jit(solution)/shard_map/ppermute | solution.py:1079
  68.7 20.5 %collective-permute-start.6 = (bf16[2,224,768]{2,1,0:T(8,128)(2,1)S(1)}, bf16[2,224,768]{2,1,0:T(8,128)(2,1)S(1)}, u32[]{:S(2)}, u32[]{:S(2)}) collective-permute-start(bf16[2,224,768]{2,1,0:T(8,128)(2,1)S(1)} %slice.215), channel_id=1, source_target_pairs={{0,1},{1,0},{2,3},{3,2},{4,5},{5,4},{6,7},{7,6},{8,9},{9,8},{10,11... | collective-permute-start | bytes 2064392 | tf_op jit(solution)/shard_map/ppermute | solution.py:1075
  89.2 5.8 %collective-permute-start.7 = (bf16[8,48,2432]{2,1,0:T(8,128)(2,1)}, bf16[8,48,2432]{2,1,0:T(8,128)(2,1)}, u32[]{:S(2)}, u32[]{:S(2)}) collective-permute-start(bf16[8,48,2432]{2,1,0:T(8,128)(2,1)} %pad_maximum_fusion.2.mine), channel_id=1, source_target_pairs={{0,2},{1,3},{2,0},{3,1},{4,6},{5,7},{6,4},{7,5},{8,10},{9,11},{10,... | collective-permute-start | bytes 5603336 | tf_op jit(solution)/shard_map/ppermute | solution.py:1075
  95.0 20.5 %collective-permute-start.8 = (bf16[24,6144]{1,0:T(8,128)(2,1)S(1)}, bf16[24,6144]{1,0:T(8,128)(2,1)S(1)}, u32[]{:S(2)}, u32[]{:S(2)}) collective-permute-start(bf16[24,6144]{1,0:T(8,128)(2,1)S(1)} %copy-done.3), channel_id=1, source_target_pairs={{0,1},{1,0},{2,3},{3,2},{4,5},{5,4},{6,7},{7,6},{8,9},{9,8},{10,11... | collective-permute-start | bytes 884744 | tf_op jit(solution)/shard_map/ppermute | solution.py:1075
  115.6 25.3 %collective-permute-start.9 = (bf16[1,48,6144]{2,1,0:T(8,128)(2,1)S(1)}, bf16[1,48,6144]{2,1,0:T(8,128)(2,1)S(1)}, u32[]{:S(2)}, u32[]{:S(2)}) collective-permute-start(bf16[1,48,6144]{2,1,0:T(8,128)(2,1)S(1)} %maximum_select_fusion.1), channel_id=1, source_target_pairs={{0,4},{1,5},{2,18},{3,19},{4,0},{5,1},{6,22},{7,23},{8,12},{9,13},... | collective-permute-start | bytes 1769480 | tf_op jit(solution)/shard_map/ppermute | solution.py:1079
  141.0 29.0 %collective-permute-start.10 = (bf16[2,48,6144]{2,1,0:T(8,128)(2,1)S(1)}, bf16[2,48,6144]{2,1,0:T(8,128)(2,1)}, u32[]{:S(2)}, u32[]{:S(2)}) collective-permute-start(bf16[2,48,6144]{2,1,0:T(8,128)(2,1)S(1)} %pad_maximum_fusion.5), channel_id=1, source_target_pairs={{0,16},{1,17},{2,10},{3,11},{4,20},{5,21},{6,14},{7,15},{8,24},{9,... | collective-permute-start | bytes 3538952 | tf_op jit(solution)/shard_map/ppermute | solution.py:1079
  171.4 50.0 %collective-permute-start.11 = (bf16[4,48,6144]{2,1,0:T(8,128)(2,1)S(1)}, bf16[4,48,6144]{2,1,0:T(8,128)(2,1)}, u32[]{:S(2)}, u32[]{:S(2)}) collective-permute-start(bf16[4,48,6144]{2,1,0:T(8,128)(2,1)S(1)} %pad_maximum_fusion.1), channel_id=1, source_target_pairs={{0,2},{1,3},{2,0},{3,1},{4,6},{5,7},{6,4},{7,5},{8,10},{9,11},{10,... | collective-permute-start | bytes 7077896 | tf_op jit(solution)/shard_map/ppermute | solution.py:1075
  183.9 37.6 %collective-permute-start.12 = (bf16[4,48,6144]{2,1,0:T(8,128)(2,1)S(1)}, bf16[4,48,6144]{2,1,0:T(8,128)(2,1)}, u32[]{:S(2)}, u32[]{:S(2)}) collective-permute-start(bf16[4,48,6144]{2,1,0:T(8,128)(2,1)S(1)} %pad_maximum_fusion.1), channel_id=1, source_target_pairs={{0,8},{1,9},{2,6},{3,7},{4,12},{5,13},{6,2},{7,3},{8,0},{9,1},{10,... | collective-permute-start | bytes 7077896 | tf_op jit(solution)/shard_map/ppermute | solution.py:1079
  183.9 37.7 %copy-start.7 = (f32[4,768]{1,0:T(4,128)S(1)}, f32[4,768]{1,0:T(4,128)}, u32[]{:S(2)}) copy-start(f32[4,768]{1,0:T(4,128)} %param.33) | copy-start | bytes 36868
  221.5 4.9 collective-permute-start.13
  252.2 275.2 %reduce-scatter.2.cloned.1.call-start = ((), (), s32[]{:S(2)}) async-start(), calls=%async_computation.3 | async-start | bytes 10948608 | tf_op jit(solution)/shard_map/reduce_scatter | solution.py:1277
  390.3 21.6 %collective-permute-start.14 = (bf16[8,48,2304]{2,1,0:T(8,128)(2,1)S(1)}, bf16[8,48,2304]{2,1,0:T(8,128)(2,1)}, u32[]{:S(2)}, u32[]{:S(2)}) collective-permute-start(bf16[8,48,2304]{2,1,0:T(8,128)(2,1)S(1)} %slice.217), channel_id=1, source_target_pairs={{0,2},{1,3},{2,0},{3,1},{4,6},{5,7},{6,4},{7,5},{8,10},{9,11},{10,... | collective-permute-start | bytes 5308424 | tf_op jit(solution)/shard_map/ppermute | solution.py:1075
  415.1 24.6 %collective-permute-start.15 = (bf16[4,48,2304]{2,1,0:T(8,128)(2,1)}, bf16[4,48,2304]{2,1,0:T(8,128)(2,1)}, u32[]{:S(2)}, u32[]{:S(2)}) collective-permute-start(bf16[4,48,2304]{2,1,0:T(8,128)(2,1)} %slice.223), channel_id=1, source_target_pairs={{0,8},{1,9},{2,6},{3,7},{4,12},{5,13},{6,2},{7,3},{8,0},{9,1},{10,... | collective-permute-start | bytes 2654216 | tf_op jit(solution)/shard_map/ppermute | solution.py:1079
  424.7 14.9 %collective-permute-start.16 = (f32[16,16,24]{2,0,1:T(8,128)S(1)}, f32[16,16,24]{2,0,1:T(8,128)S(1)}, u32[]{:S(2)}, u32[]{:S(2)}) collective-permute-start(f32[16,16,24]{2,0,1:T(8,128)S(1)} %slice_select_fusion), channel_id=1, source_target_pairs={{0,16},{1,17},{2,18},{3,19},{4,20},{5,21},{6,22},{7,23},{8,24},{9,... | collective-permute-start | bytes 73736 | tf_op jit(solution)/shard_map/ppermute | solution.py:1075
  430.6 24.2 %collective-permute-start.17 = (bf16[2,176,768]{2,1,0:T(8,128)(2,1)}, bf16[2,176,768]{2,1,0:T(8,128)(2,1)S(1)}, u32[]{:S(2)}, u32[]{:S(2)}) collective-permute-start(bf16[2,176,768]{2,1,0:T(8,128)(2,1)} %get-tuple-element.319), channel_id=1, source_target_pairs={{0,1},{1,0},{2,3},{3,2},{4,5},{5,4},{6,7},{7,6},{8,9},{9,8},{10,11... | collective-permute-start | bytes 1622024 | tf_op jit(solution)/shard_map/ppermute | solution.py:1075
  433.8 41.0 %collective-permute-start.20 = (bf16[2,160,768]{2,1,0:T(8,128)(2,1)}, bf16[2,160,768]{2,1,0:T(8,128)(2,1)}, u32[]{:S(2)}, u32[]{:S(2)}) collective-permute-start(bf16[2,160,768]{2,1,0:T(8,128)(2,1)} %slice.231), channel_id=1, source_target_pairs={{0,1},{1,0},{2,3},{3,2},{4,5},{5,4},{6,7},{7,6},{8,9},{9,8},{10,11... | collective-permute-start | bytes 1474568 | tf_op jit(solution)/shard_map/ppermute | solution.py:1075
  455.9 6.4 %collective-permute-start.19 = (f32[8,16,24]{2,0,1:T(8,128)S(1)}, f32[8,16,24]{2,0,1:T(8,128)S(1)}, u32[]{:S(2)}, u32[]{:S(2)}) collective-permute-start(f32[8,16,24]{2,0,1:T(8,128)S(1)} %slice_select_fusion.1), channel_id=1, source_target_pairs={{0,8},{1,9},{2,10},{3,11},{4,12},{5,13},{6,14},{7,15},{8,0},{9,1},... | collective-permute-start | bytes 36872 | tf_op jit(solution)/shard_map/ppermute | solution.py:1075
  456.0 18.8 %collective-permute-start.18 = (bf16[2,48,2304]{2,1,0:T(8,128)(2,1)S(1)}, bf16[2,48,2304]{2,1,0:T(8,128)(2,1)S(1)}, u32[]{:S(2)}, u32[]{:S(2)}) collective-permute-start(bf16[2,48,2304]{2,1,0:T(8,128)(2,1)S(1)} %slice.228), channel_id=1, source_target_pairs={{0,16},{1,17},{2,10},{3,11},{4,20},{5,21},{6,14},{7,15},{8,24},{9,... | collective-permute-start | bytes 1327112 | tf_op jit(solution)/shard_map/ppermute | solution.py:1079
  474.8 40.0 %copy-start.2 = (f32[24,3072]{1,0:T(8,128)S(1)}, f32[24,3072]{1,0:T(8,128)}, u32[]{:S(2)}) copy-start(f32[24,3072]{1,0:T(8,128)} %get-tuple-element.248) | copy-start | bytes 884740
  474.9 26.6 %collective-permute-start.22 = (f32[4,16,24]{2,0,1:T(4,128)S(1)}, f32[4,16,24]{2,0,1:T(4,128)S(1)}, u32[]{:S(2)}, u32[]{:S(2)}) collective-permute-start(f32[4,16,24]{2,0,1:T(4,128)S(1)} %slice_select_fusion.2), channel_id=1, source_target_pairs={{0,4},{1,5},{2,6},{3,7},{4,0},{5,1},{6,2},{7,3},{8,12},{9,13},{10,... | collective-permute-start | bytes 18440 | tf_op jit(solution)/shard_map/ppermute | solution.py:1075
  500.2 9.6 %collective-permute-start.23 = (bf16[2,176,768]{2,1,0:T(8,128)(2,1)}, bf16[2,176,768]{2,1,0:T(8,128)(2,1)S(1)}, u32[]{:S(2)}, u32[]{:S(2)}) collective-permute-start(bf16[2,176,768]{2,1,0:T(8,128)(2,1)} %get-tuple-element.318), channel_id=1, source_target_pairs={{0,1},{1,0},{2,3},{3,2},{4,5},{5,4},{6,7},{7,6},{8,9},{9,8},{10,11... | collective-permute-start | bytes 1622024 | tf_op jit(solution)/shard_map/ppermute | solution.py:1075
  500.2 6.0 %collective-permute-start.21 = (bf16[1,48,2304]{2,1,0:T(8,128)(2,1)S(1)}, bf16[1,48,2304]{2,1,0:T(8,128)(2,1)S(1)}, u32[]{:S(2)}, u32[]{:S(2)}) collective-permute-start(bf16[1,48,2304]{2,1,0:T(8,128)(2,1)S(1)} %slice.241), channel_id=1, source_target_pairs={{0,4},{1,5},{2,18},{3,19},{4,0},{5,1},{6,22},{7,23},{8,12},{9,13},... | collective-permute-start | bytes 663560 | tf_op jit(solution)/shard_map/ppermute | solution.py:1079
  509.8 1.2 collective-permute-start.24
  510.4 16.3 %collective-permute-start.26 = (bf16[1,24,2304]{2,1,0:T(8,128)(2,1)S(1)}, bf16[1,24,2304]{2,1,0:T(8,128)(2,1)S(1)}, u32[]{:S(2)}, u32[]{:S(2)}) collective-permute-start(bf16[1,24,2304]{2,1,0:T(8,128)(2,1)S(1)} %broadcast_select_fusion), channel_id=1, source_target_pairs={{0,1},{1,0},{2,3},{3,2},{4,5},{5,4},{6,7},{7,6},{8,9},{9,8},{10,11... | collective-permute-start | bytes 331784 | tf_op jit(solution)/shard_map/ppermute | solution.py:1075
  511.1 14.4 %collective-permute-start.25 = (f32[1,16,24]{2,0,1:T(1,128)S(1)}, f32[1,16,24]{2,0,1:T(1,128)S(1)}, u32[]{:S(2)}, u32[]{:S(2)}) collective-permute-start(f32[1,16,24]{2,0,1:T(1,128)S(1)} %broadcast_select_fusion.2), channel_id=1, source_target_pairs={{0,1},{1,0},{2,3},{3,2},{4,5},{5,4},{6,7},{7,6},{8,9},{9,8},{10,11... | collective-permute-start | bytes 4616 | tf_op jit(solution)/shard_map/ppermute | solution.py:1075
  (9 other events, 73.5 us)
Sparse Core Ops, SparseCore 0:
  13.9 145.6 all-gather.2
  252.3 68.6 all-gather.4
  327.2 165.8 reduce-scatter.1
